TPU v7x, 32 devices: a whole 2x2x4 slice. The times are simulated.
32 devices in a mesh: emb: 8 (over z, y), seq: 4 (over x, core).
Axes of the slice: x: 2, y: 2, z: 4, core: 2. Of those that a mesh axis runs over, the one named last changes fastest.
Arguments:
- item_table: bfloat16 [32768, 512], P(('emb', 'seq')), may hold values from -6 to 6
- unique_ids: int32 [2048], P(('emb', 'seq')), may hold values from 0 to 32767, as said below
- inverse: int32 [256, 256], P(('emb', 'seq')), may hold values from 0 to 63, as said below
- lengths: int32 [256], P(('emb', 'seq')), may hold values from 64 to 256, as said below
- assignment: int32 [256], P(('emb', 'seq')), may hold values from 0 to 31, as said below
- proj_in: bfloat16 [512, 2048], replicated, may hold values from -0.25 to 0.25
- bias_in: float32 [2048], replicated, may hold values from -3 to 3
- gain_in: float32 [512], replicated, may hold values from 0.1 to 1.9
- gain_mid: float32 [512], replicated, may hold values from 0.1 to 1.9
- proj_out: bfloat16 [512, 512], replicated, may hold values from -0.25 to 0.25
- position_bias: float32 [4, 256], replicated, may hold values from -4 to 4
- cotangent: bfloat16 [256, 256, 512], P(('emb', 'seq')), may hold values from -6 to 6
Outputs:
- outputs: bfloat16 [256, 256, 512], P(('emb', 'seq'))
- table_grad: float32 [32768, 512], P(('emb', 'seq'))
Inputs may be any that keep to these rules, and one draw needn't show every extreme that they name: `unique_ids`: each device's 64 entries are distinct row numbers; row r is held by device r // 1024; a device names at most 4 rows held by any one device, and exactly 4 of some device. `inverse`: every entry of a device's unique list is named by some token at a position below its slot's length. `lengths`: every group of 4 devices along seq has a slot of length 256. `assignment`: value v of a slot of a device with emb index e places it in slot v % 8 of the device with emb index e and seq index v // 8. Within a group it is a permutation, and the slots that the device with seq index s sends to a device take that device's slots s * 2 to (s + 1) * 2 - 1.
All inputs are finite; a program needn't handle non-finite values.
Results may differ from a plain program's by a relative error of at most 0.015.
Values may be sent and summed in bfloat16 or wider, within the bound.
A program may use at most 64 MiB of HBM per device.

v0:
```python
import jax
import jax.numpy as jnp
from jax import lax
from jax.sharding import PartitionSpec as P


def layer_norm(values, gain):
    center = values - jnp.mean(values, axis=-1, keepdims=True)
    spread = jnp.mean(center * center, axis=-1, keepdims=True)
    return center * lax.rsqrt(spread + 1e-05) * gain


def relative_table(position_bias, length):
    head_count = position_bias.shape[0]
    first = jnp.broadcast_to(position_bias[:, :1], (head_count, length + 1))
    wrapped = jnp.concatenate([first, position_bias[:, :0:-1]], axis=1)
    tiled = jnp.tile(wrapped, (1, length))[:, : length * (2 * length - 1)]
    return tiled.reshape(head_count, length, 2 * length - 1)[:, :, :length]


def slot_layer(inputs, seq_len, proj_in, bias_in, gain_in, gain_mid, proj_out, toeplitz):
    length = inputs.shape[0]
    feature = inputs.shape[1]
    head_count = toeplitz.shape[0]
    head_size = feature // head_count
    normed = layer_norm(inputs.astype(jnp.float32), gain_in).astype(jnp.bfloat16)
    hidden = jax.nn.silu(
        jnp.dot(normed, proj_in, preferred_element_type=jnp.float32) + bias_in
    ).astype(jnp.bfloat16)
    gate_portion = hidden[:, :feature]
    value_part = hidden[:, feature : 2 * feature].reshape(length, head_count, head_size)
    query_part = hidden[:, 2 * feature : 3 * feature].reshape(length, head_count, head_size)
    key_part = hidden[:, 3 * feature :].reshape(length, head_count, head_size)
    scores = (
        jnp.einsum("ihe,jhe->hij", query_part, key_part, preferred_element_type=jnp.float32)
        * head_size ** (-0.5)
        + toeplitz
    )
    row_pos = jnp.arange(length, dtype=jnp.int32)[:, None]
    col_pos = jnp.arange(length, dtype=jnp.int32)[None, :]
    allowed = (col_pos <= row_pos) & (row_pos < seq_len)
    weights = jnp.where(
        allowed[None], jax.nn.silu(scores) / seq_len.astype(jnp.float32), 0.0
    ).astype(jnp.bfloat16)
    mixed_heads = jnp.einsum(
        "hij,jhe->ihe", weights, value_part, preferred_element_type=jnp.float32
    ).reshape(length, feature)
    gated_out = (layer_norm(mixed_heads, gain_mid) * gate_portion.astype(jnp.float32)).astype(
        jnp.bfloat16
    )
    result = inputs.astype(jnp.float32) + jnp.dot(
        gated_out, proj_out, preferred_element_type=jnp.float32
    )
    return jnp.where(row_pos < seq_len, result, 0.0).astype(jnp.bfloat16)


def slot_step(slot_in, seq_len, grad_out, proj_in, bias_in, gain_in, gain_mid, proj_out, toeplitz):
    result, pullback = jax.vjp(
        lambda inputs: slot_layer(
            inputs, seq_len, proj_in, bias_in, gain_in, gain_mid, proj_out, toeplitz
        ),
        slot_in,
    )
    return (result, pullback(grad_out)[0])


def selector(ids, in_range, width):
    columns = jnp.arange(width, dtype=jnp.int32)
    return ((ids[:, :, None] == columns[None, None, :]) & in_range[:, :, None]).astype(jnp.bfloat16)


def shards(
    item_table,
    unique_ids,
    inverse,
    lengths,
    assignment,
    proj_in,
    bias_in,
    gain_in,
    gain_mid,
    proj_out,
    position_bias,
    cotangent,
):
    emb_count = lax.axis_size("emb")
    seq_count = lax.axis_size("seq")
    devices = emb_count * seq_count
    rows_dev = item_table.shape[0]
    feature = item_table.shape[1]
    unique_count = unique_ids.shape[0]
    slot_cap = 2 * unique_count // devices
    owners = unique_ids // rows_dev
    local_row = unique_ids % rows_dev
    matches = (owners[:, None] == jnp.arange(devices, dtype=jnp.int32)[None, :]).astype(jnp.int32)
    running = jnp.cumsum(matches, axis=0)
    slot_rank = jnp.sum(running * matches, axis=1) - 1
    request = (
        jnp.full((devices, slot_cap), rows_dev, jnp.int32).at[owners, slot_rank].set(local_row)
    )
    asked = lax.all_to_all(request, ("emb", "seq"), split_axis=0, concat_axis=0, tiled=True)
    answer = lax.all_to_all(
        item_table[jnp.minimum(asked, rows_dev - 1)],
        ("emb", "seq"),
        split_axis=0,
        concat_axis=0,
        tiled=True,
    )
    distinct_item_rows = answer[owners, slot_rank]
    slot_count = lengths.shape[0]
    per_partner = slot_count // seq_count
    max_len = inverse.shape[1]
    bucket = assignment // slot_count * per_partner + assignment % per_partner
    chosen = (
        jnp.zeros((slot_count,), jnp.int32).at[bucket].set(jnp.arange(slot_count, dtype=jnp.int32))
    )
    sent_ids = inverse[chosen]
    sent_len = lengths[chosen]
    position = jnp.arange(max_len, dtype=jnp.int32)
    toeplitz = relative_table(position_bias, max_len)
    shared = lax.all_gather(distinct_item_rows, "seq", axis=0, tiled=True)
    got_ids, count_totals = (
        lax.all_to_all(
            sent_ids.reshape(seq_count, per_partner, max_len),
            "seq",
            split_axis=0,
            concat_axis=0,
            tiled=True,
        ),
        lax.all_to_all(
            sent_len.reshape(seq_count, per_partner), "seq", split_axis=0, concat_axis=0, tiled=True
        ),
    )
    count_totals = count_totals.reshape(slot_count)
    source = jnp.arange(slot_count, dtype=jnp.int32) // per_partner
    shared_ids = got_ids.reshape(slot_count, max_len) + (source * unique_count)[:, None]
    in_range = position[None, :] < count_totals[:, None]
    row_chooser = selector(shared_ids, in_range, seq_count * unique_count)
    balanced = jnp.einsum(
        "gmq,qp->gmp", row_chooser, shared, preferred_element_type=jnp.float32
    ).astype(jnp.bfloat16)
    outputs, token_grads = lax.map(
        lambda packed: slot_step(
            packed[0], packed[1], packed[2], proj_in, bias_in, gain_in, gain_mid, proj_out, toeplitz
        ),
        (balanced, count_totals, cotangent),
    )
    partial_sums = jnp.einsum(
        "ehm,ehr->mr", row_chooser, token_grads, preferred_element_type=jnp.float32
    )
    row_gradient_list = lax.psum_scatter(
        partial_sums.astype(jnp.bfloat16), "seq", scatter_dimension=0, tiled=True
    ).astype(jnp.float32)
    outgoing_grads = (
        jnp.zeros((devices, slot_cap, feature), jnp.float32)
        .at[owners, slot_rank]
        .set(row_gradient_list)
    )
    landed = lax.all_to_all(
        outgoing_grads.astype(jnp.bfloat16), ("emb", "seq"), split_axis=0, concat_axis=0, tiled=True
    ).astype(outgoing_grads.dtype)
    table_grad = (
        jnp.zeros((rows_dev, feature), jnp.float32)
        .at[asked.reshape(-1)]
        .add(landed.reshape(-1, feature), mode="drop")
    )
    return (outputs, table_grad)


def solution(mesh):
    in_specs = (
        P(("emb", "seq"), None),
        P(("emb", "seq")),
        P(("emb", "seq"), None),
        P(("emb", "seq")),
        P(("emb", "seq")),
        P(),
        P(),
        P(),
        P(),
        P(),
        P(),
        P(("emb", "seq"), None, None),
    )
    out_specs = (P(("emb", "seq"), None, None), P(("emb", "seq"), None))
    return jax.shard_map(shards, mesh=mesh, in_specs=in_specs, out_specs=out_specs, check_vma=False)
```

profile of v0, /device:TPU:0, one launch (start us, length us, event | category | flops | bytes accessed | tf_op | source)
XLA Modules:
  0.0 369.1 jit_solution(15471484370043388460)
XLA Ops:
  10.6 4.2 %all-to-all-start = ((s32[4,1,2]{2,1,0:T(1,128)}), s32[4,1,2]{2,1,0:T(1,128)S(1)}, u32[]{:S(2)}, u32[]{:S(2)}) async-start(s32[4,1,2]{2,1,0:T(1,128)} %bitcast.16), calls=%async_computation | async-start | bytes 4096 | tf_op jit(solution)/shard_map/all_to_all | solution.py:130
  17.4 3.5 scatter_fusion
  22.2 6.8 %all-to-all-start.2 = ((s32[32,1,4]{2,1,0:T(1,128)}), s32[32,1,4]{2,1,0:T(1,128)S(1)}, u32[]{:S(2)}, u32[]{:S(2)}) async-start(s32[32,1,4]{2,1,0:T(1,128)} %copy.74), calls=%async_computation.2 | async-start | bytes 32768 | tf_op jit(solution)/shard_map/all_to_all | solution.py:101
  31.8 3.6 reshape.278
  39.0 3.2 all-to-all-start.1
  46.0 4.9 %all-to-all-start.3 = ((bf16[32,4,512]{2,1,0:T(4,128)(2,1)}), bf16[32,4,512]{2,1,0:T(4,128)(2,1)S(1)}, u32[]{:S(2)}, u32[]{:S(2)}) async-start(bf16[32,4,512]{2,1,0:T(4,128)(2,1)} %reshape.302), calls=%async_computation.3 | async-start | bytes 262144 | tf_op jit(solution)/shard_map/all_to_all | solution.py:102
  51.1 8.0 %all-to-all-done.3 = bf16[32,4,512]{2,1,0:T(4,128)(2,1)S(1)} async-done(((bf16[32,4,512]{2,1,0:T(4,128)(2,1)}), bf16[32,4,512]{2,1,0:T(4,128)(2,1)S(1)}, u32[]{:S(2)}, u32[]{:S(2)}) %all-to-all-start.3) | async-done | bytes 131104 | tf_op jit(solution)/shard_map/all_to_all | solution.py:102
  60.1 6.0 %all_gather.3 = bf16[256,512]{1,0:T(8,128)(2,1)S(1)} all-gather(bf16[64,512]{1,0:T(8,128)(2,1)S(1)} %gather_fusion.3), channel_id=1, replica_groups=mesh['emb'=8,'seq'=4] {'seq'}, dimensions={0}, use_global_device_ids=true | all-gather | bytes 327680 | tf_op jit(solution)/shard_map/all_gather | solution.py:121
  68.2 252.5 %while.12 = (s32[]{:T(128)}, bf16[8,256,512]{2,1,0:T(8,128)(2,1)}, bf16[8,256,512]{2,1,0:T(8,128)(2,1)}, s32[8]{0:T(128)S(1)}, bf16[8,256,512]{2,1,0:T(8,128)(2,...) while((s32[]{:T(128)}, bf16[8,256,512]{2,1,0:T(8,128)(2,1)}, ...), condition=%wide.region_13.14_spmd, body=%wide.region_4.13_spmd.sunk | while | flops 1773407488 | bytes 45614620 | solution.py:142
  70.5 3.9 %multiply_convert_fusion.3 = (bf16[256,2048]{1,0:T(8,128)(2,1)S(1)}, f32[256,2048]{1,0:T(8,128)}) fusion(f32[2048]{0:T(1024)S(1)} %get-tuple-element.255, bf16[512,2048]{1,0:T(8,128)(2,1)} %get-tuple-element.254, f32[512]{0:T(512)S(1)} %get-tuple-element.253, f32[256]{0:T(256)S(1)} %fusion.178, f32[256]{0:T(256)S(1)} %broadcast_multiply_fusion.4, ...), kind=kOutput, calls=%fused_computation.15.clone.1 | convolution fusion | flops 540672000 | bytes 5517824 | tf_op jit(solution)/shard_map/while/body/eval_jaxpr/jvp()/dot_general | solution.py:28
  90.9 3.4 fusion.187
  102.0 3.9 %multiply_convert_fusion.3 = (bf16[256,2048]{1,0:T(8,128)(2,1)S(1)}, f32[256,2048]{1,0:T(8,128)}) fusion(f32[2048]{0:T(1024)S(1)} %get-tuple-element.255, bf16[512,2048]{1,0:T(8,128)(2,1)} %get-tuple-element.254, f32[512]{0:T(512)S(1)} %get-tuple-element.253, f32[256]{0:T(256)S(1)} %fusion.178, f32[256]{0:T(256)S(1)} %broadcast_multiply_fusion.4, ...), kind=kOutput, calls=%fused_computation.15.clone.1 | convolution fusion | flops 540672000 | bytes 5517824 | tf_op jit(solution)/shard_map/while/body/eval_jaxpr/jvp()/dot_general | solution.py:28
  109.1 2.8 select_convert_fusion.2
  122.5 3.4 fusion.187
  133.6 3.9 %multiply_convert_fusion.3 = (bf16[256,2048]{1,0:T(8,128)(2,1)S(1)}, f32[256,2048]{1,0:T(8,128)}) fusion(f32[2048]{0:T(1024)S(1)} %get-tuple-element.255, bf16[512,2048]{1,0:T(8,128)(2,1)} %get-tuple-element.254, f32[512]{0:T(512)S(1)} %get-tuple-element.253, f32[256]{0:T(256)S(1)} %fusion.178, f32[256]{0:T(256)S(1)} %broadcast_multiply_fusion.4, ...), kind=kOutput, calls=%fused_computation.15.clone.1 | convolution fusion | flops 540672000 | bytes 5517824 | tf_op jit(solution)/shard_map/while/body/eval_jaxpr/jvp()/dot_general | solution.py:28
  140.7 2.8 select_convert_fusion.2
  154.0 3.4 fusion.187
  165.1 3.9 %multiply_convert_fusion.3 = (bf16[256,2048]{1,0:T(8,128)(2,1)S(1)}, f32[256,2048]{1,0:T(8,128)}) fusion(f32[2048]{0:T(1024)S(1)} %get-tuple-element.255, bf16[512,2048]{1,0:T(8,128)(2,1)} %get-tuple-element.254, f32[512]{0:T(512)S(1)} %get-tuple-element.253, f32[256]{0:T(256)S(1)} %fusion.178, f32[256]{0:T(256)S(1)} %broadcast_multiply_fusion.4, ...), kind=kOutput, calls=%fused_computation.15.clone.1 | convolution fusion | flops 540672000 | bytes 5517824 | tf_op jit(solution)/shard_map/while/body/eval_jaxpr/jvp()/dot_general | solution.py:28
  185.6 3.4 fusion.187
  196.7 3.9 %multiply_convert_fusion.3 = (bf16[256,2048]{1,0:T(8,128)(2,1)S(1)}, f32[256,2048]{1,0:T(8,128)}) fusion(f32[2048]{0:T(1024)S(1)} %get-tuple-element.255, bf16[512,2048]{1,0:T(8,128)(2,1)} %get-tuple-element.254, f32[512]{0:T(512)S(1)} %get-tuple-element.253, f32[256]{0:T(256)S(1)} %fusion.178, f32[256]{0:T(256)S(1)} %broadcast_multiply_fusion.4, ...), kind=kOutput, calls=%fused_computation.15.clone.1 | convolution fusion | flops 540672000 | bytes 5517824 | tf_op jit(solution)/shard_map/while/body/eval_jaxpr/jvp()/dot_general | solution.py:28
  217.1 3.4 fusion.187
  228.3 3.9 %multiply_convert_fusion.3 = (bf16[256,2048]{1,0:T(8,128)(2,1)S(1)}, f32[256,2048]{1,0:T(8,128)}) fusion(f32[2048]{0:T(1024)S(1)} %get-tuple-element.255, bf16[512,2048]{1,0:T(8,128)(2,1)} %get-tuple-element.254, f32[512]{0:T(512)S(1)} %get-tuple-element.253, f32[256]{0:T(256)S(1)} %fusion.178, f32[256]{0:T(256)S(1)} %broadcast_multiply_fusion.4, ...), kind=kOutput, calls=%fused_computation.15.clone.1 | convolution fusion | flops 540672000 | bytes 5517824 | tf_op jit(solution)/shard_map/while/body/eval_jaxpr/jvp()/dot_general | solution.py:28
  248.7 3.4 fusion.187
  259.8 3.9 %multiply_convert_fusion.3 = (bf16[256,2048]{1,0:T(8,128)(2,1)S(1)}, f32[256,2048]{1,0:T(8,128)}) fusion(f32[2048]{0:T(1024)S(1)} %get-tuple-element.255, bf16[512,2048]{1,0:T(8,128)(2,1)} %get-tuple-element.254, f32[512]{0:T(512)S(1)} %get-tuple-element.253, f32[256]{0:T(256)S(1)} %fusion.178, f32[256]{0:T(256)S(1)} %broadcast_multiply_fusion.4, ...), kind=kOutput, calls=%fused_computation.15.clone.1 | convolution fusion | flops 540672000 | bytes 5517824 | tf_op jit(solution)/shard_map/while/body/eval_jaxpr/jvp()/dot_general | solution.py:28
  280.3 3.4 fusion.187
  291.4 3.9 %multiply_convert_fusion.3 = (bf16[256,2048]{1,0:T(8,128)(2,1)S(1)}, f32[256,2048]{1,0:T(8,128)}) fusion(f32[2048]{0:T(1024)S(1)} %get-tuple-element.255, bf16[512,2048]{1,0:T(8,128)(2,1)} %get-tuple-element.254, f32[512]{0:T(512)S(1)} %get-tuple-element.253, f32[256]{0:T(256)S(1)} %fusion.178, f32[256]{0:T(256)S(1)} %broadcast_multiply_fusion.4, ...), kind=kOutput, calls=%fused_computation.15.clone.1 | convolution fusion | flops 540672000 | bytes 5517824 | tf_op jit(solution)/shard_map/while/body/eval_jaxpr/jvp()/dot_general | solution.py:28
  311.8 3.4 fusion.187
  320.7 3.0 fusion.90
  323.7 17.6 %reduce-scatter.2.cloned.1.call-done = bf16[64,512]{1,0:T(8,128)(2,1)} async-done(((bf16[256,512]{1,0:T(8,128)(2,1)}), bf16[64,512]{1,0:T(8,128)(2,1)}) %reduce-scatter.2.cloned.1.call-update) | async-done | bytes 65552 | tf_op jit(solution)/shard_map/reduce_scatter | solution.py:151
  342.2 3.7 %scatter_fusion.1 = f32[32,4,512]{2,1,0:T(4,128)S(1)} fusion(f32[32,4,512]{2,1,0:T(4,128)S(1)} %broadcast_in_dim.100, s32[64]{0:T(128)S(1)} %get-tuple-element.110, f32[64,512]{1,0:T(8,128)S(1)} %convert_element_type.102), kind=kCustom, calls=%fused_computation.6 | custom fusion | bytes 393728 | tf_op jit(solution)/shard_map/scatter | solution.py:157
  346.6 4.6 %all-to-all-start.4 = ((bf16[32,4,512]{2,1,0:T(4,128)(2,1)}), bf16[32,4,512]{2,1,0:T(4,128)(2,1)S(1)}, u32[]{:S(2)}, u32[]{:S(2)}) async-start(bf16[32,4,512]{2,1,0:T(4,128)(2,1)} %convert_element_type.103), calls=%async_computation.5 | async-start | bytes 262144 | tf_op jit(solution)/shard_map/all_to_all | solution.py:159
  352.0 7.4 %all-to-all-done.4 = bf16[32,4,512]{2,1,0:T(4,128)(2,1)S(1)} async-done(((bf16[32,4,512]{2,1,0:T(4,128)(2,1)}), bf16[32,4,512]{2,1,0:T(4,128)(2,1)S(1)}, u32[]{:S(2)}, u32[]{:S(2)}) %all-to-all-start.4) | async-done | bytes 131104 | tf_op jit(solution)/shard_map/all_to_all | solution.py:159
  (393 shorter events, 208.0 us)
Async XLA Ops:
  7.2 35.4 %copy-start = (bf16[1024,512]{1,0:T(8,128)(2,1)S(1)}, bf16[1024,512]{1,0:T(8,128)(2,1)}, u32[]{:S(2)}) copy-start(bf16[1024,512]{1,0:T(8,128)(2,1)} %param.14) | copy-start | bytes 3145732
  7.2 21.9 %copy-start.5 = (s32[8,256]{1,0:T(8,128)S(1)}, s32[8,256]{1,0:T(8,128)}, u32[]{:S(2)}) copy-start(s32[8,256]{1,0:T(8,128)} %param.16) | copy-start | bytes 24580
  10.6 11.7 %all-to-all-start = ((s32[4,1,2]{2,1,0:T(1,128)}), s32[4,1,2]{2,1,0:T(1,128)S(1)}, u32[]{:S(2)}, u32[]{:S(2)}) async-start(s32[4,1,2]{2,1,0:T(1,128)} %bitcast.16), calls=%async_computation | async-start | bytes 4096 | tf_op jit(solution)/shard_map/all_to_all | solution.py:130
  22.2 16.8 %all-to-all-start.2 = ((s32[32,1,4]{2,1,0:T(1,128)}), s32[32,1,4]{2,1,0:T(1,128)S(1)}, u32[]{:S(2)}, u32[]{:S(2)}) async-start(s32[32,1,4]{2,1,0:T(1,128)} %copy.74), calls=%async_computation.2 | async-start | bytes 32768 | tf_op jit(solution)/shard_map/all_to_all | solution.py:101
  39.0 7.0 %all-to-all-start.1 = ((s32[4,2,256]{2,1,0:T(2,128)}), s32[4,2,256]{2,1,0:T(2,128)S(1)}, u32[]{:S(2)}, u32[]{:S(2)}) async-start(s32[4,2,256]{2,1,0:T(2,128)} %reshape.276), calls=%async_computation.1 | async-start | bytes 16384 | tf_op jit(solution)/shard_map/all_to_all | solution.py:123
  43.4 24.8 %copy-start.6 = (f32[512]{0:T(512)S(1)}, f32[512]{0:T(512)}, u32[]{:S(2)}) copy-start(f32[512]{0:T(512)} %param.22) | copy-start | bytes 6148
  43.4 24.8 %copy-start.7 = (f32[2048]{0:T(1024)S(1)}, f32[2048]{0:T(1024)}, u32[]{:S(2)}) copy-start(f32[2048]{0:T(1024)} %param.20) | copy-start | bytes 24580
  43.4 24.8 %copy-start.8 = (f32[512]{0:T(512)S(1)}, f32[512]{0:T(512)}, u32[]{:S(2)}) copy-start(f32[512]{0:T(512)} %param.21) | copy-start | bytes 6148
  46.0 13.2 %all-to-all-start.3 = ((bf16[32,4,512]{2,1,0:T(4,128)(2,1)}), bf16[32,4,512]{2,1,0:T(4,128)(2,1)S(1)}, u32[]{:S(2)}, u32[]{:S(2)}) async-start(bf16[32,4,512]{2,1,0:T(4,128)(2,1)} %reshape.302), calls=%async_computation.3 | async-start | bytes 262144 | tf_op jit(solution)/shard_map/all_to_all | solution.py:102
  50.9 290.4 %reduce-scatter.2.cloned.1.call-start = ((), (), s32[]{:S(2)}) async-start(), calls=%async_computation.6 | async-start | bytes 327680 | tf_op jit(solution)/shard_map/reduce_scatter | solution.py:151
  74.3 1.0 copy-start.1
  75.4 5.0 %copy-start.2 = (bf16[32,4,8,128]{3,2,1,0:T(8,128)(2,1)}, bf16[32,4,8,128]{3,2,1,0:T(8,128)(2,1)S(1)}, u32[]{:S(2)}) copy-start(bf16[32,4,8,128]{3,2,1,0:T(8,128)(2,1)S(1)} %get-tuple-element.208) | copy-start | bytes 786436 | tf_op jit(solution)/shard_map/while
  94.3 3.3 copy-start.3
  105.9 1.0 copy-start.1
  107.0 5.0 %copy-start.2 = (bf16[32,4,8,128]{3,2,1,0:T(8,128)(2,1)}, bf16[32,4,8,128]{3,2,1,0:T(8,128)(2,1)S(1)}, u32[]{:S(2)}) copy-start(bf16[32,4,8,128]{3,2,1,0:T(8,128)(2,1)S(1)} %get-tuple-element.208) | copy-start | bytes 786436 | tf_op jit(solution)/shard_map/while
  125.9 3.3 copy-start.3
  137.5 1.0 copy-start.1
  138.5 5.0 %copy-start.2 = (bf16[32,4,8,128]{3,2,1,0:T(8,128)(2,1)}, bf16[32,4,8,128]{3,2,1,0:T(8,128)(2,1)S(1)}, u32[]{:S(2)}) copy-start(bf16[32,4,8,128]{3,2,1,0:T(8,128)(2,1)S(1)} %get-tuple-element.208) | copy-start | bytes 786436 | tf_op jit(solution)/shard_map/while
  157.5 3.3 copy-start.3
  170.1 5.0 %copy-start.2 = (bf16[32,4,8,128]{3,2,1,0:T(8,128)(2,1)}, bf16[32,4,8,128]{3,2,1,0:T(8,128)(2,1)S(1)}, u32[]{:S(2)}) copy-start(bf16[32,4,8,128]{3,2,1,0:T(8,128)(2,1)S(1)} %get-tuple-element.208) | copy-start | bytes 786436 | tf_op jit(solution)/shard_map/while
  189.0 3.3 copy-start.3
  200.6 1.0 copy-start.1
  201.7 5.0 %copy-start.2 = (bf16[32,4,8,128]{3,2,1,0:T(8,128)(2,1)}, bf16[32,4,8,128]{3,2,1,0:T(8,128)(2,1)S(1)}, u32[]{:S(2)}) copy-start(bf16[32,4,8,128]{3,2,1,0:T(8,128)(2,1)S(1)} %get-tuple-element.208) | copy-start | bytes 786436 | tf_op jit(solution)/shard_map/while
  220.6 3.3 copy-start.3
  232.1 1.0 copy-start.1
  233.2 5.0 %copy-start.2 = (bf16[32,4,8,128]{3,2,1,0:T(8,128)(2,1)}, bf16[32,4,8,128]{3,2,1,0:T(8,128)(2,1)S(1)}, u32[]{:S(2)}) copy-start(bf16[32,4,8,128]{3,2,1,0:T(8,128)(2,1)S(1)} %get-tuple-element.208) | copy-start | bytes 786436 | tf_op jit(solution)/shard_map/while
  252.1 3.3 copy-start.3
  264.8 5.0 %copy-start.2 = (bf16[32,4,8,128]{3,2,1,0:T(8,128)(2,1)}, bf16[32,4,8,128]{3,2,1,0:T(8,128)(2,1)S(1)}, u32[]{:S(2)}) copy-start(bf16[32,4,8,128]{3,2,1,0:T(8,128)(2,1)S(1)} %get-tuple-element.208) | copy-start | bytes 786436 | tf_op jit(solution)/shard_map/while
  283.7 3.3 copy-start.3
  296.3 5.0 %copy-start.2 = (bf16[32,4,8,128]{3,2,1,0:T(8,128)(2,1)}, bf16[32,4,8,128]{3,2,1,0:T(8,128)(2,1)S(1)}, u32[]{:S(2)}) copy-start(bf16[32,4,8,128]{3,2,1,0:T(8,128)(2,1)S(1)} %get-tuple-element.208) | copy-start | bytes 786436 | tf_op jit(solution)/shard_map/while
  315.3 3.3 copy-start.3
  346.6 12.8 %all-to-all-start.4 = ((bf16[32,4,512]{2,1,0:T(4,128)(2,1)}), bf16[32,4,512]{2,1,0:T(4,128)(2,1)S(1)}, u32[]{:S(2)}, u32[]{:S(2)}) async-start(bf16[32,4,512]{2,1,0:T(4,128)(2,1)} %convert_element_type.103), calls=%async_computation.5 | async-start | bytes 262144 | tf_op jit(solution)/shard_map/all_to_all | solution.py:159
  (11 other events, 10.7 us)
Sparse Core Ops, SparseCore 0:
  323.8 17.3 reduce-scatter.1
where the time goes:
time: 373 us; the launch traced here: 369 us
  matrix products  147 us (39%)
  other arithmetic  74.7 us (20%)
  local copies, waits for them, and re-layouts  62.7 us (17%)
  waiting for transfers between devices  35 us (9%)
  starting transfers between devices  23.8 us (6%)
  between operations  14.3 us (4%)
  loops' own time  6.02 us (2%)
  blocking collectives  5.97 us (2%)
    dot_general x16, matrix products, slot_layer(): jnp.dot(normed, proj_in, preferred_element_type=jnp.float32) + bias_in  58.5 us
    reduce_sum x24, other arithmetic, layer_norm(): center = values - jnp.mean(values, axis=-1, keepdims=True)  34.1 us
    dot_general x24, matrix products, slot_layer(): jnp.einsum('ihe,jhe->hij', query_part, key_part, preferred_element_type=j...  32.4 us
    dot_general x16, matrix products, slot_layer(): jnp.dot(gated_out, proj_out, preferred_element_type=jnp.float32)  30 us
    dot_general x24, matrix products, slot_layer(): jnp.einsum('hij,jhe->ihe', weights, value_part, preferred_element_type=jn...  20.5 us
    reduce_scatter x1, waiting for transfers between devices, shards(): lax.psum_scatter(partial_sums.astype(jnp.bfloat16), 'seq', scatter_dimens...  17.6 us
    dynamic_update_slice x8, other arithmetic, shards(): lax.map(lambda packed: slot_step(packed[0], packed[1], packed[2], proj_in...  16.1 us
    reshape x16, local copies, waits for them, and re-layouts, slot_layer(): key_part = hidden[:, 3 * feature:].reshape(length, head_count, head_size)  15.4 us
  transfers between devices with their start and end apart: 6, of which 4 were waited for; matrix products, arithmetic and copies ran while one was open for 5% of the time, Pallas kernels for 0%

commit v1 on v0

--- a/solution.py
+++ b/solution.py
@@ -92,9 +92,9 @@
     slot_cap = 2 * unique_count // devices
     owners = unique_ids // rows_dev
     local_row = unique_ids % rows_dev
-    matches = (owners[:, None] == jnp.arange(devices, dtype=jnp.int32)[None, :]).astype(jnp.int32)
-    running = jnp.cumsum(matches, axis=0)
-    slot_rank = jnp.sum(running * matches, axis=1) - 1
+    order = jnp.arange(unique_count, dtype=jnp.int32)
+    earlier = (owners[:, None] == owners[None, :]) & (order[None, :] < order[:, None])
+    slot_rank = jnp.sum(earlier.astype(jnp.int32), axis=1)
     request = (
         jnp.full((devices, slot_cap), rows_dev, jnp.int32).at[owners, slot_rank].set(local_row)
     )

time: 373 us -> 372 us (level)
  no operation moved by 1% of the time
where the time goes in v1:
time: 372 us; the launch traced here: 369 us
  matrix products  147 us (40%)
  other arithmetic  74.5 us (20%)
  local copies, waits for them, and re-layouts  62.7 us (17%)
  waiting for transfers between devices  34.9 us (9%)
  starting transfers between devices  23.9 us (6%)
  between operations  14.3 us (4%)
  loops' own time  6.02 us (2%)
  blocking collectives  5.97 us (2%)
    dot_general x16, matrix products, slot_layer(): jnp.dot(normed, proj_in, preferred_element_type=jnp.float32) + bias_in  58.5 us
    reduce_sum x24, other arithmetic, layer_norm(): center = values - jnp.mean(values, axis=-1, keepdims=True)  34.1 us
    dot_general x24, matrix products, slot_layer(): jnp.einsum('ihe,jhe->hij', query_part, key_part, preferred_element_type=j...  32.4 us
    dot_general x16, matrix products, slot_layer(): jnp.dot(gated_out, proj_out, preferred_element_type=jnp.float32)  30 us
    dot_general x24, matrix products, slot_layer(): jnp.einsum('hij,jhe->ihe', weights, value_part, preferred_element_type=jn...  20.5 us
    reduce_scatter x1, waiting for transfers between devices, shards(): lax.psum_scatter(partial_sums.astype(jnp.bfloat16), 'seq', scatter_dimens...  17.5 us
    dynamic_update_slice x8, other arithmetic, shards(): lax.map(lambda packed: slot_step(packed[0], packed[1], packed[2], proj_in...  16.1 us
    reshape x16, local copies, waits for them, and re-layouts, slot_layer(): key_part = hidden[:, 3 * feature:].reshape(length, head_count, head_size)  15.4 us
  transfers between devices with their start and end apart: 6, of which 4 were waited for; matrix products, arithmetic and copies ran while one was open for 5% of the time, Pallas kernels for 0%

profile of v1, /device:TPU:0, one launch (start us, length us, event | category | flops | bytes accessed | tf_op | source)
XLA Modules:
  0.0 368.9 jit_solution(15807715079937676910)
XLA Ops:
  10.6 4.2 %all-to-all-start = ((s32[4,1,2]{2,1,0:T(1,128)}), s32[4,1,2]{2,1,0:T(1,128)S(1)}, u32[]{:S(2)}, u32[]{:S(2)}) async-start(s32[4,1,2]{2,1,0:T(1,128)} %bitcast.16), calls=%async_computation | async-start | bytes 4096 | tf_op jit(solution)/shard_map/all_to_all | solution.py:130
  17.2 3.5 scatter_fusion
  22.1 6.8 %all-to-all-start.2 = ((s32[32,1,4]{2,1,0:T(1,128)}), s32[32,1,4]{2,1,0:T(1,128)S(1)}, u32[]{:S(2)}, u32[]{:S(2)}) async-start(s32[32,1,4]{2,1,0:T(1,128)} %copy.91), calls=%async_computation.2 | async-start | bytes 32768 | tf_op jit(solution)/shard_map/all_to_all | solution.py:101
  31.6 3.6 reshape.272
  38.8 3.2 all-to-all-start.1
  45.8 4.9 %all-to-all-start.3 = ((bf16[32,4,512]{2,1,0:T(4,128)(2,1)}), bf16[32,4,512]{2,1,0:T(4,128)(2,1)S(1)}, u32[]{:S(2)}, u32[]{:S(2)}) async-start(bf16[32,4,512]{2,1,0:T(4,128)(2,1)} %reshape.296), calls=%async_computation.3 | async-start | bytes 262144 | tf_op jit(solution)/shard_map/all_to_all | solution.py:102
  51.0 8.0 %all-to-all-done.3 = bf16[32,4,512]{2,1,0:T(4,128)(2,1)S(1)} async-done(((bf16[32,4,512]{2,1,0:T(4,128)(2,1)}), bf16[32,4,512]{2,1,0:T(4,128)(2,1)S(1)}, u32[]{:S(2)}, u32[]{:S(2)}) %all-to-all-start.3) | async-done | bytes 131104 | tf_op jit(solution)/shard_map/all_to_all | solution.py:102
  59.9 6.0 %all_gather.3 = bf16[256,512]{1,0:T(8,128)(2,1)S(1)} all-gather(bf16[64,512]{1,0:T(8,128)(2,1)S(1)} %gather_fusion.3), channel_id=1, replica_groups=mesh['emb'=8,'seq'=4] {'seq'}, dimensions={0}, use_global_device_ids=true | all-gather | bytes 327680 | tf_op jit(solution)/shard_map/all_gather | solution.py:121
  68.0 252.5 %while.12 = (s32[]{:T(128)}, bf16[8,256,512]{2,1,0:T(8,128)(2,1)}, bf16[8,256,512]{2,1,0:T(8,128)(2,1)}, s32[8]{0:T(128)S(1)}, bf16[8,256,512]{2,1,0:T(8,128)(2,...) while((s32[]{:T(128)}, bf16[8,256,512]{2,1,0:T(8,128)(2,1)}, ...), condition=%wide.region_12.13_spmd, body=%wide.region_3.12_spmd.sunk | while | flops 1773407488 | bytes 45614620 | solution.py:142
  70.3 3.9 %multiply_convert_fusion.3 = (bf16[256,2048]{1,0:T(8,128)(2,1)S(1)}, f32[256,2048]{1,0:T(8,128)}) fusion(f32[2048]{0:T(1024)S(1)} %get-tuple-element.255, bf16[512,2048]{1,0:T(8,128)(2,1)} %get-tuple-element.254, f32[512]{0:T(512)S(1)} %get-tuple-element.253, f32[256]{0:T(256)S(1)} %fusion.178, f32[256]{0:T(256)S(1)} %broadcast_multiply_fusion.4, ...), kind=kOutput, calls=%fused_computation.15.clone.1 | convolution fusion | flops 540672000 | bytes 5517824 | tf_op jit(solution)/shard_map/while/body/eval_jaxpr/jvp()/dot_general | solution.py:28
  90.7 3.4 fusion.187
  101.8 3.9 %multiply_convert_fusion.3 = (bf16[256,2048]{1,0:T(8,128)(2,1)S(1)}, f32[256,2048]{1,0:T(8,128)}) fusion(f32[2048]{0:T(1024)S(1)} %get-tuple-element.255, bf16[512,2048]{1,0:T(8,128)(2,1)} %get-tuple-element.254, f32[512]{0:T(512)S(1)} %get-tuple-element.253, f32[256]{0:T(256)S(1)} %fusion.178, f32[256]{0:T(256)S(1)} %broadcast_multiply_fusion.4, ...), kind=kOutput, calls=%fused_computation.15.clone.1 | convolution fusion | flops 540672000 | bytes 5517824 | tf_op jit(solution)/shard_map/while/body/eval_jaxpr/jvp()/dot_general | solution.py:28
  108.9 2.8 select_convert_fusion.2
  122.3 3.4 fusion.187
  133.4 3.9 %multiply_convert_fusion.3 = (bf16[256,2048]{1,0:T(8,128)(2,1)S(1)}, f32[256,2048]{1,0:T(8,128)}) fusion(f32[2048]{0:T(1024)S(1)} %get-tuple-element.255, bf16[512,2048]{1,0:T(8,128)(2,1)} %get-tuple-element.254, f32[512]{0:T(512)S(1)} %get-tuple-element.253, f32[256]{0:T(256)S(1)} %fusion.178, f32[256]{0:T(256)S(1)} %broadcast_multiply_fusion.4, ...), kind=kOutput, calls=%fused_computation.15.clone.1 | convolution fusion | flops 540672000 | bytes 5517824 | tf_op jit(solution)/shard_map/while/body/eval_jaxpr/jvp()/dot_general | solution.py:28
  140.5 2.8 select_convert_fusion.2
  153.8 3.4 fusion.187
  165.0 3.9 %multiply_convert_fusion.3 = (bf16[256,2048]{1,0:T(8,128)(2,1)S(1)}, f32[256,2048]{1,0:T(8,128)}) fusion(f32[2048]{0:T(1024)S(1)} %get-tuple-element.255, bf16[512,2048]{1,0:T(8,128)(2,1)} %get-tuple-element.254, f32[512]{0:T(512)S(1)} %get-tuple-element.253, f32[256]{0:T(256)S(1)} %fusion.178, f32[256]{0:T(256)S(1)} %broadcast_multiply_fusion.4, ...), kind=kOutput, calls=%fused_computation.15.clone.1 | convolution fusion | flops 540672000 | bytes 5517824 | tf_op jit(solution)/shard_map/while/body/eval_jaxpr/jvp()/dot_general | solution.py:28
  185.4 3.4 fusion.187
  196.5 3.9 %multiply_convert_fusion.3 = (bf16[256,2048]{1,0:T(8,128)(2,1)S(1)}, f32[256,2048]{1,0:T(8,128)}) fusion(f32[2048]{0:T(1024)S(1)} %get-tuple-element.255, bf16[512,2048]{1,0:T(8,128)(2,1)} %get-tuple-element.254, f32[512]{0:T(512)S(1)} %get-tuple-element.253, f32[256]{0:T(256)S(1)} %fusion.178, f32[256]{0:T(256)S(1)} %broadcast_multiply_fusion.4, ...), kind=kOutput, calls=%fused_computation.15.clone.1 | convolution fusion | flops 540672000 | bytes 5517824 | tf_op jit(solution)/shard_map/while/body/eval_jaxpr/jvp()/dot_general | solution.py:28
  217.0 3.4 fusion.187
  228.1 3.9 %multiply_convert_fusion.3 = (bf16[256,2048]{1,0:T(8,128)(2,1)S(1)}, f32[256,2048]{1,0:T(8,128)}) fusion(f32[2048]{0:T(1024)S(1)} %get-tuple-element.255, bf16[512,2048]{1,0:T(8,128)(2,1)} %get-tuple-element.254, f32[512]{0:T(512)S(1)} %get-tuple-element.253, f32[256]{0:T(256)S(1)} %fusion.178, f32[256]{0:T(256)S(1)} %broadcast_multiply_fusion.4, ...), kind=kOutput, calls=%fused_computation.15.clone.1 | convolution fusion | flops 540672000 | bytes 5517824 | tf_op jit(solution)/shard_map/while/body/eval_jaxpr/jvp()/dot_general | solution.py:28
  248.5 3.4 fusion.187
  259.7 3.9 %multiply_convert_fusion.3 = (bf16[256,2048]{1,0:T(8,128)(2,1)S(1)}, f32[256,2048]{1,0:T(8,128)}) fusion(f32[2048]{0:T(1024)S(1)} %get-tuple-element.255, bf16[512,2048]{1,0:T(8,128)(2,1)} %get-tuple-element.254, f32[512]{0:T(512)S(1)} %get-tuple-element.253, f32[256]{0:T(256)S(1)} %fusion.178, f32[256]{0:T(256)S(1)} %broadcast_multiply_fusion.4, ...), kind=kOutput, calls=%fused_computation.15.clone.1 | convolution fusion | flops 540672000 | bytes 5517824 | tf_op jit(solution)/shard_map/while/body/eval_jaxpr/jvp()/dot_general | solution.py:28
  280.1 3.4 fusion.187
  291.2 3.9 %multiply_convert_fusion.3 = (bf16[256,2048]{1,0:T(8,128)(2,1)S(1)}, f32[256,2048]{1,0:T(8,128)}) fusion(f32[2048]{0:T(1024)S(1)} %get-tuple-element.255, bf16[512,2048]{1,0:T(8,128)(2,1)} %get-tuple-element.254, f32[512]{0:T(512)S(1)} %get-tuple-element.253, f32[256]{0:T(256)S(1)} %fusion.178, f32[256]{0:T(256)S(1)} %broadcast_multiply_fusion.4, ...), kind=kOutput, calls=%fused_computation.15.clone.1 | convolution fusion | flops 540672000 | bytes 5517824 | tf_op jit(solution)/shard_map/while/body/eval_jaxpr/jvp()/dot_general | solution.py:28
  311.6 3.4 fusion.187
  320.5 3.0 fusion.90
  323.6 17.5 %reduce-scatter.2.cloned.1.call-done = bf16[64,512]{1,0:T(8,128)(2,1)} async-done(((bf16[256,512]{1,0:T(8,128)(2,1)}), bf16[64,512]{1,0:T(8,128)(2,1)}) %reduce-scatter.2.cloned.1.call-update) | async-done | bytes 65552 | tf_op jit(solution)/shard_map/reduce_scatter | solution.py:151
  342.0 3.7 %scatter_fusion.1 = f32[32,4,512]{2,1,0:T(4,128)S(1)} fusion(f32[32,4,512]{2,1,0:T(4,128)S(1)} %broadcast_in_dim.102, s32[64]{0:T(128)S(1)} %get-tuple-element.110, f32[64,512]{1,0:T(8,128)S(1)} %convert_element_type.102), kind=kCustom, calls=%fused_computation.6 | custom fusion | bytes 393728 | tf_op jit(solution)/shard_map/scatter | solution.py:157
  346.4 4.6 %all-to-all-start.4 = ((bf16[32,4,512]{2,1,0:T(4,128)(2,1)}), bf16[32,4,512]{2,1,0:T(4,128)(2,1)S(1)}, u32[]{:S(2)}, u32[]{:S(2)}) async-start(bf16[32,4,512]{2,1,0:T(4,128)(2,1)} %convert_element_type.103), calls=%async_computation.5 | async-start | bytes 262144 | tf_op jit(solution)/shard_map/all_to_all | solution.py:159
  351.8 7.4 %all-to-all-done.4 = bf16[32,4,512]{2,1,0:T(4,128)(2,1)S(1)} async-done(((bf16[32,4,512]{2,1,0:T(4,128)(2,1)}), bf16[32,4,512]{2,1,0:T(4,128)(2,1)S(1)}, u32[]{:S(2)}, u32[]{:S(2)}) %all-to-all-start.4) | async-done | bytes 131104 | tf_op jit(solution)/shard_map/all_to_all | solution.py:159
  (391 shorter events, 207.8 us)
Async XLA Ops:
  7.2 35.2 %copy-start = (bf16[1024,512]{1,0:T(8,128)(2,1)S(1)}, bf16[1024,512]{1,0:T(8,128)(2,1)}, u32[]{:S(2)}) copy-start(bf16[1024,512]{1,0:T(8,128)(2,1)} %param.14) | copy-start | bytes 3145732
  7.2 21.7 %copy-start.5 = (s32[8,256]{1,0:T(8,128)S(1)}, s32[8,256]{1,0:T(8,128)}, u32[]{:S(2)}) copy-start(s32[8,256]{1,0:T(8,128)} %param.16) | copy-start | bytes 24580
  10.6 11.5 %all-to-all-start = ((s32[4,1,2]{2,1,0:T(1,128)}), s32[4,1,2]{2,1,0:T(1,128)S(1)}, u32[]{:S(2)}, u32[]{:S(2)}) async-start(s32[4,1,2]{2,1,0:T(1,128)} %bitcast.16), calls=%async_computation | async-start | bytes 4096 | tf_op jit(solution)/shard_map/all_to_all | solution.py:130
  22.1 16.8 %all-to-all-start.2 = ((s32[32,1,4]{2,1,0:T(1,128)}), s32[32,1,4]{2,1,0:T(1,128)S(1)}, u32[]{:S(2)}, u32[]{:S(2)}) async-start(s32[32,1,4]{2,1,0:T(1,128)} %copy.91), calls=%async_computation.2 | async-start | bytes 32768 | tf_op jit(solution)/shard_map/all_to_all | solution.py:101
  38.8 7.0 %all-to-all-start.1 = ((s32[4,2,256]{2,1,0:T(2,128)}), s32[4,2,256]{2,1,0:T(2,128)S(1)}, u32[]{:S(2)}, u32[]{:S(2)}) async-start(s32[4,2,256]{2,1,0:T(2,128)} %reshape.270), calls=%async_computation.1 | async-start | bytes 16384 | tf_op jit(solution)/shard_map/all_to_all | solution.py:123
  43.2 24.8 %copy-start.6 = (f32[512]{0:T(512)S(1)}, f32[512]{0:T(512)}, u32[]{:S(2)}) copy-start(f32[512]{0:T(512)} %param.22) | copy-start | bytes 6148
  43.2 24.8 %copy-start.7 = (f32[2048]{0:T(1024)S(1)}, f32[2048]{0:T(1024)}, u32[]{:S(2)}) copy-start(f32[2048]{0:T(1024)} %param.20) | copy-start | bytes 24580
  43.2 24.8 %copy-start.8 = (f32[512]{0:T(512)S(1)}, f32[512]{0:T(512)}, u32[]{:S(2)}) copy-start(f32[512]{0:T(512)} %param.21) | copy-start | bytes 6148
  45.8 13.2 %all-to-all-start.3 = ((bf16[32,4,512]{2,1,0:T(4,128)(2,1)}), bf16[32,4,512]{2,1,0:T(4,128)(2,1)S(1)}, u32[]{:S(2)}, u32[]{:S(2)}) async-start(bf16[32,4,512]{2,1,0:T(4,128)(2,1)} %reshape.296), calls=%async_computation.3 | async-start | bytes 262144 | tf_op jit(solution)/shard_map/all_to_all | solution.py:102
  50.8 290.3 %reduce-scatter.2.cloned.1.call-start = ((), (), s32[]{:S(2)}) async-start(), calls=%async_computation.6 | async-start | bytes 327680 | tf_op jit(solution)/shard_map/reduce_scatter | solution.py:151
  75.2 5.0 %copy-start.2 = (bf16[32,4,8,128]{3,2,1,0:T(8,128)(2,1)}, bf16[32,4,8,128]{3,2,1,0:T(8,128)(2,1)S(1)}, u32[]{:S(2)}) copy-start(bf16[32,4,8,128]{3,2,1,0:T(8,128)(2,1)S(1)} %get-tuple-element.208) | copy-start | bytes 786436 | tf_op jit(solution)/shard_map/while
  94.2 3.3 copy-start.3
  105.7 1.0 copy-start.1
  106.8 5.0 %copy-start.2 = (bf16[32,4,8,128]{3,2,1,0:T(8,128)(2,1)}, bf16[32,4,8,128]{3,2,1,0:T(8,128)(2,1)S(1)}, u32[]{:S(2)}) copy-start(bf16[32,4,8,128]{3,2,1,0:T(8,128)(2,1)S(1)} %get-tuple-element.208) | copy-start | bytes 786436 | tf_op jit(solution)/shard_map/while
  125.7 3.3 copy-start.3
  137.3 1.0 copy-start.1
  138.4 5.0 %copy-start.2 = (bf16[32,4,8,128]{3,2,1,0:T(8,128)(2,1)}, bf16[32,4,8,128]{3,2,1,0:T(8,128)(2,1)S(1)}, u32[]{:S(2)}) copy-start(bf16[32,4,8,128]{3,2,1,0:T(8,128)(2,1)S(1)} %get-tuple-element.208) | copy-start | bytes 786436 | tf_op jit(solution)/shard_map/while
  157.3 3.3 copy-start.3
  168.8 1.0 copy-start.1
  169.9 5.0 %copy-start.2 = (bf16[32,4,8,128]{3,2,1,0:T(8,128)(2,1)}, bf16[32,4,8,128]{3,2,1,0:T(8,128)(2,1)S(1)}, u32[]{:S(2)}) copy-start(bf16[32,4,8,128]{3,2,1,0:T(8,128)(2,1)S(1)} %get-tuple-element.208) | copy-start | bytes 786436 | tf_op jit(solution)/shard_map/while
  188.8 3.3 copy-start.3
  200.4 1.0 copy-start.1
  201.5 5.0 %copy-start.2 = (bf16[32,4,8,128]{3,2,1,0:T(8,128)(2,1)}, bf16[32,4,8,128]{3,2,1,0:T(8,128)(2,1)S(1)}, u32[]{:S(2)}) copy-start(bf16[32,4,8,128]{3,2,1,0:T(8,128)(2,1)S(1)} %get-tuple-element.208) | copy-start | bytes 786436 | tf_op jit(solution)/shard_map/while
  220.4 3.3 copy-start.3
  232.0 1.0 copy-start.1
  233.0 5.0 %copy-start.2 = (bf16[32,4,8,128]{3,2,1,0:T(8,128)(2,1)}, bf16[32,4,8,128]{3,2,1,0:T(8,128)(2,1)S(1)}, u32[]{:S(2)}) copy-start(bf16[32,4,8,128]{3,2,1,0:T(8,128)(2,1)S(1)} %get-tuple-element.208) | copy-start | bytes 786436 | tf_op jit(solution)/shard_map/while
  252.0 3.3 copy-start.3
  264.6 5.0 %copy-start.2 = (bf16[32,4,8,128]{3,2,1,0:T(8,128)(2,1)}, bf16[32,4,8,128]{3,2,1,0:T(8,128)(2,1)S(1)}, u32[]{:S(2)}) copy-start(bf16[32,4,8,128]{3,2,1,0:T(8,128)(2,1)S(1)} %get-tuple-element.208) | copy-start | bytes 786436 | tf_op jit(solution)/shard_map/while
  283.5 3.3 copy-start.3
  296.2 5.0 %copy-start.2 = (bf16[32,4,8,128]{3,2,1,0:T(8,128)(2,1)}, bf16[32,4,8,128]{3,2,1,0:T(8,128)(2,1)S(1)}, u32[]{:S(2)}) copy-start(bf16[32,4,8,128]{3,2,1,0:T(8,128)(2,1)S(1)} %get-tuple-element.208) | copy-start | bytes 786436 | tf_op jit(solution)/shard_map/while
  315.1 3.3 copy-start.3
  346.4 12.9 %all-to-all-start.4 = ((bf16[32,4,512]{2,1,0:T(4,128)(2,1)}), bf16[32,4,512]{2,1,0:T(4,128)(2,1)S(1)}, u32[]{:S(2)}, u32[]{:S(2)}) async-start(bf16[32,4,512]{2,1,0:T(4,128)(2,1)} %convert_element_type.103), calls=%async_computation.5 | async-start | bytes 262144 | tf_op jit(solution)/shard_map/all_to_all | solution.py:159
  (11 other events, 10.7 us)
Sparse Core Ops, SparseCore 0:
  323.7 17.3 reduce-scatter.1

commit v2 on v1

v2 whole, which is shorter than its diff:
```python
import functools

import jax
import jax.numpy as jnp
from jax import lax
from jax.experimental import pallas as pl
from jax.experimental.pallas import tpu as pltpu
from jax.sharding import PartitionSpec as P


def nn(a, b):
    return lax.dot_general(a, b, (((1,), (0,)), ((), ())), preferred_element_type=jnp.float32)


def nt(a, b):
    return lax.dot_general(a, b, (((1,), (1,)), ((), ())), preferred_element_type=jnp.float32)


def tn(a, b):
    return lax.dot_general(a, b, (((0,), (0,)), ((), ())), preferred_element_type=jnp.float32)


def silu_parts(values):
    gate = 0.5 * jnp.tanh(0.5 * values) + 0.5
    out = values * gate
    return out, gate + out * (1.0 - gate)


def norm_parts(values):
    center = values - jnp.mean(values, axis=-1, keepdims=True)
    spread = jnp.mean(center * center, axis=-1, keepdims=True)
    scale = lax.rsqrt(spread + 1e-05)
    return center * scale, scale


def norm_pull(grad, unit, scale):
    first = jnp.mean(grad, axis=-1, keepdims=True)
    second = jnp.mean(grad * unit, axis=-1, keepdims=True)
    return scale * (grad - first - unit * second)


def layer_kernel(
    per_source,
    unique_count,
    sel_ref,
    len_ref,
    ids_ref,
    shared_ref,
    cot_ref,
    proj_in_ref,
    bias_in_ref,
    gain_in_ref,
    gain_mid_ref,
    proj_out_ref,
    rev_ref,
    out_ref,
    part_ref,
    table,
    acc,
    hidden,
    slope,
    weights,
    wslope,
    mixed,
    dpre,
):
    step = pl.program_id(0)
    head_count, max_len = rev_ref.shape
    feature = shared_ref.shape[1]
    head = feature // head_count
    width = shared_ref.shape[0]
    root = head ** (-0.5)
    count = len_ref[step]

    @pl.when(step == 0)
    def _():
        acc[...] = jnp.zeros_like(acc)
        for h in range(head_count):
            row = jnp.broadcast_to(rev_ref[h : h + 1, :], (max_len, max_len))
            table[h] = pltpu.roll(row, 0, 1, stride=1, stride_axis=0)

    def run(rows):
        ids = ids_ref[0, :, :rows] + sel_ref[step] // per_source * unique_count
        place = lax.broadcasted_iota(jnp.int32, (1, rows), 1)
        ids = jnp.where(place < count, ids, -1)
        chooser = jnp.where(
            lax.broadcasted_iota(jnp.int32, (width, rows), 0) == ids, 1.0, 0.0
        ).astype(jnp.bfloat16)
        valid = lax.broadcasted_iota(jnp.int32, (rows, 1), 0) < count
        inputs = tn(chooser, shared_ref[...])
        unit_in, scale_in = norm_parts(inputs)
        normed = (unit_in * gain_in_ref[...]).astype(jnp.bfloat16)
        for c in range(4):
            cols = slice(c * feature, (c + 1) * feature)
            value, rate = silu_parts(nn(normed, proj_in_ref[:, cols]) + bias_in_ref[:, cols])
            hidden[:rows, cols] = value.astype(jnp.bfloat16)
            slope[:rows, cols] = rate.astype(jnp.bfloat16)
        causal = lax.broadcasted_iota(jnp.int32, (rows, rows), 1) <= lax.broadcasted_iota(
            jnp.int32, (rows, rows), 0
        )
        share = 1.0 / jnp.full((1, 1), count, jnp.int32).astype(jnp.float32)

        def part(c, h):
            return slice(c * feature + h * head, c * feature + (h + 1) * head)

        for h in range(head_count):
            score = nt(hidden[:rows, part(2, h)], hidden[:rows, part(3, h)]) * root
            value, rate = silu_parts(score + table[h, :rows, :rows])
            weight = jnp.where(causal, value * share, 0.0).astype(jnp.bfloat16)
            weights[h, :rows, :rows] = weight
            wslope[h, :rows, :rows] = jnp.where(causal, rate * share, 0.0).astype(jnp.bfloat16)
            mixed[:rows, part(0, h)] = nn(weight, hidden[:rows, part(1, h)])
        unit_mid, scale_mid = norm_parts(mixed[:rows, :])
        normed_mid = unit_mid * gain_mid_ref[...]
        gate = hidden[:rows, :feature].astype(jnp.float32)
        gated = (normed_mid * gate).astype(jnp.bfloat16)
        result = inputs + nn(gated, proj_out_ref[...])
        out_ref[0, :rows, :] = jnp.where(valid, result, 0.0).astype(jnp.bfloat16)
        if rows < max_len:
            out_ref[0, rows:, :] = jnp.zeros((max_len - rows, feature), jnp.bfloat16)

        grad = jnp.where(valid, cot_ref[0, :rows, :].astype(jnp.float32), 0.0)
        grad_gated = nt(grad.astype(jnp.bfloat16), proj_out_ref[...])
        grad_gated = grad_gated.astype(jnp.bfloat16).astype(jnp.float32)

        def put(cols, value):
            value = value.astype(jnp.bfloat16).astype(jnp.float32)
            dpre[:rows, cols] = (value * slope[:rows, cols].astype(jnp.float32)).astype(
                jnp.bfloat16
            )

        put(slice(0, feature), grad_gated * normed_mid)
        grad_mixed = norm_pull(grad_gated * gate * gain_mid_ref[...], unit_mid, scale_mid)
        grad_mixed = grad_mixed.astype(jnp.bfloat16)
        for h in range(head_count):
            grad_head = grad_mixed[:, h * head : (h + 1) * head]
            put(part(1, h), tn(weights[h, :rows, :rows], grad_head))
            grad_weight = nt(grad_head, hidden[:rows, part(1, h)])
            grad_score = (grad_weight * wslope[h, :rows, :rows].astype(jnp.float32)).astype(
                jnp.bfloat16
            )
            put(part(2, h), nn(grad_score, hidden[:rows, part(3, h)]) * root)
            put(part(3, h), tn(grad_score, hidden[:rows, part(2, h)]) * root)
        grad_normed = nt(dpre[:rows, :], proj_in_ref[...])
        grad_normed = grad_normed.astype(jnp.bfloat16).astype(jnp.float32)
        grad_in = norm_pull(grad_normed * gain_in_ref[...], unit_in, scale_in)
        token_grad = (grad_in.astype(jnp.bfloat16).astype(jnp.float32) + grad).astype(jnp.bfloat16)
        acc[...] += nn(chooser, token_grad)

    half = max_len // 2

    @pl.when(count <= half)
    def _():
        run(half)

    @pl.when(count > half)
    def _():
        run(max_len)

    @pl.when(step == pl.num_programs(0) - 1)
    def _():
        part_ref[...] = acc[...].astype(part_ref.dtype)


def layers(
    selected, counts, ids, shared, cotangent, proj_in, bias_in, gain_in, gain_mid, proj_out, position_bias, per_source, unique_count
):
    slots, max_len, feature = cotangent.shape
    heads = position_bias.shape[0]
    width = shared.shape[0]
    rev = jnp.concatenate([position_bias[:, :1], position_bias[:, :0:-1]], axis=1)
    whole = lambda shape: pl.BlockSpec(shape, lambda t, sel, n: (0,) * len(shape))
    slot = pl.BlockSpec((1, max_len, feature), lambda t, sel, n: (t, 0, 0))
    return pl.pallas_call(
        functools.partial(layer_kernel, per_source, unique_count),
        grid_spec=pltpu.PrefetchScalarGridSpec(
            num_scalar_prefetch=2,
            grid=(slots,),
            in_specs=[
                pl.BlockSpec((1, 1, max_len), lambda t, sel, n: (sel[t], 0, 0)),
                whole((width, feature)),
                slot,
                whole(proj_in.shape),
                whole((1, bias_in.shape[0])),
                whole((1, feature)),
                whole((1, feature)),
                whole(proj_out.shape),
                whole((heads, max_len)),
            ],
            out_specs=[slot, whole((width, feature))],
            scratch_shapes=[
                pltpu.VMEM((heads, max_len, max_len), jnp.float32),
                pltpu.VMEM((width, feature), jnp.float32),
                pltpu.VMEM((max_len, 4 * feature), jnp.bfloat16),
                pltpu.VMEM((max_len, 4 * feature), jnp.bfloat16),
                pltpu.VMEM((heads, max_len, max_len), jnp.bfloat16),
                pltpu.VMEM((heads, max_len, max_len), jnp.bfloat16),
                pltpu.VMEM((max_len, feature), jnp.float32),
                pltpu.VMEM((max_len, 4 * feature), jnp.bfloat16),
            ],
        ),
        out_shape=[
            jax.ShapeDtypeStruct((slots, max_len, feature), jnp.bfloat16),
            jax.ShapeDtypeStruct((width, feature), jnp.bfloat16),
        ],
        compiler_params=pltpu.CompilerParams(
            dimension_semantics=("arbitrary",), vmem_limit_bytes=48 * 1024 * 1024
        ),
    )(
        selected, counts, ids.reshape(ids.shape[0], 1, max_len), shared, cotangent,
        proj_in, bias_in[None], gain_in[None], gain_mid[None], proj_out, rev,
    )


def shards(
    item_table,
    unique_ids,
    inverse,
    lengths,
    assignment,
    proj_in,
    bias_in,
    gain_in,
    gain_mid,
    proj_out,
    position_bias,
    cotangent,
):
    emb_count = lax.axis_size("emb")
    seq_count = lax.axis_size("seq")
    devices = emb_count * seq_count
    rows_dev = item_table.shape[0]
    feature = item_table.shape[1]
    unique_count = unique_ids.shape[0]
    slot_cap = 2 * unique_count // devices
    owners = unique_ids // rows_dev
    local_row = unique_ids % rows_dev
    order = jnp.arange(unique_count, dtype=jnp.int32)
    earlier = (owners[:, None] == owners[None, :]) & (order[None, :] < order[:, None])
    slot_rank = jnp.sum(earlier.astype(jnp.int32), axis=1)
    request = (
        jnp.full((devices, slot_cap), rows_dev, jnp.int32).at[owners, slot_rank].set(local_row)
    )
    asked = lax.all_to_all(request, ("emb", "seq"), split_axis=0, concat_axis=0, tiled=True)
    answer = lax.all_to_all(
        item_table[jnp.minimum(asked, rows_dev - 1)],
        ("emb", "seq"),
        split_axis=0,
        concat_axis=0,
        tiled=True,
    )
    distinct_item_rows = answer[owners, slot_rank]
    slot_count = lengths.shape[0]
    max_len = inverse.shape[1]
    packed = jnp.concatenate([inverse, lengths[:, None], assignment[:, None]], axis=1)
    group = lax.all_gather(packed, "seq", axis=0, tiled=True)
    group_ids = group[:, :max_len]
    group_len = group[:, max_len]
    mine = lax.axis_index("seq") * slot_count + jnp.arange(slot_count, dtype=jnp.int32)
    hit = (group[:, max_len + 1][None, :] == mine[:, None]).astype(jnp.int32)
    selected = jnp.sum(hit * jnp.arange(hit.shape[1], dtype=jnp.int32)[None, :], axis=1)
    counts = jnp.sum(hit * group_len[None, :], axis=1)
    shared = lax.all_gather(distinct_item_rows, "seq", axis=0, tiled=True)
    outputs, partial_sums = layers(
        selected, counts, group_ids, shared, cotangent, proj_in, bias_in, gain_in, gain_mid,
        proj_out, position_bias, slot_count, unique_count,
    )
    pieces = lax.all_to_all(partial_sums, "seq", split_axis=0, concat_axis=0, tiled=True)
    row_gradient_list = jnp.sum(
        pieces.reshape(seq_count, unique_count, feature).astype(jnp.float32), axis=0
    )
    outgoing_grads = (
        jnp.zeros((devices, slot_cap, feature), jnp.float32)
        .at[owners, slot_rank]
        .set(row_gradient_list)
    )
    landed = lax.all_to_all(
        outgoing_grads.astype(jnp.bfloat16), ("emb", "seq"), split_axis=0, concat_axis=0, tiled=True
    ).astype(outgoing_grads.dtype)
    table_grad = (
        jnp.zeros((rows_dev, feature), jnp.float32)
        .at[asked.reshape(-1)]
        .add(landed.reshape(-1, feature), mode="drop")
    )
    return (outputs, table_grad)


def solution(mesh):
    in_specs = (
        P(("emb", "seq"), None),
        P(("emb", "seq")),
        P(("emb", "seq"), None),
        P(("emb", "seq")),
        P(("emb", "seq")),
        P(),
        P(),
        P(),
        P(),
        P(),
        P(),
        P(("emb", "seq"), None, None),
    )
    out_specs = (P(("emb", "seq"), None, None), P(("emb", "seq"), None))
    return jax.shard_map(shards, mesh=mesh, in_specs=in_specs, out_specs=out_specs, check_vma=False)
```

time: 372 us -> 106 us (0.28)
  matrix products: 147 us -> 0 us
  other arithmetic: 74.5 us -> 6.19 us
  local copies, waits for them, and re-layouts: 62.7 us -> 17.4 us
  Pallas kernels: 0 us -> 36.7 us
  waiting for transfers between devices: 34.9 us -> 12.4 us
  between operations: 14.3 us -> 0.82 us
  blocking collectives: 5.97 us -> 19.4 us
  starting transfers between devices: 23.9 us -> 12.7 us
  loops' own time: 6.02 us -> 0 us
    dot_general x82 -> x0, matrix products: 147 us -> none  [the longest x16 58.5 us: slot_layer(): jnp.dot(normed, proj_in, preferred_element_type=jnp.float32) + bias_in]
    reduce_sum x40 -> x2, other arithmetic: 44.3 us -> 0.22 us  [the longest x1 0.18 us: shards(): counts = jnp.sum(hit * group_len[None, :], axis=1)]
    pallas_call x0 -> x1, Pallas kernels: none -> 36.7 us  [layers(): pl.pallas_call(functools.partial(layer_kernel, per_source, unique_count),...]
    reshape x59 -> x1, local copies, waits for them, and re-layouts: 25.6 us -> 0.03 us  [layers(): ids.reshape(ids.shape[0], 1, max_len)]
    reduce_scatter x1 -> x0, waiting for transfers between devices: 17.5 us -> none  [shards(): lax.psum_scatter(partial_sums.astype(jnp.bfloat16), 'seq', scatter_dimens...]
    dynamic_update_slice x8 -> x0, other arithmetic: 16.1 us -> none  [shards(): lax.map(lambda packed: slot_step(packed[0], packed[1], packed[2], proj_in...]
    while x72 -> x0, local copies, waits for them, and re-layouts: 11.9 us -> none
    all_to_all x0 -> x1, blocking collectives: none -> 8.41 us  [shards(): lax.all_to_all(partial_sums, 'seq', split_axis=0, concat_axis=0, tiled=True)]
  transfers between devices with their start and end apart: 6 -> 3, of which waited for: 4 -> 3; matrix products, arithmetic and copies ran while one was open for 5% -> 6% of each run, Pallas kernels for 0% -> 0%
where the time goes in v2:
time: 106 us
  Pallas kernels  36.7 us (35%)
  blocking collectives  19.4 us (18%)
  local copies, waits for them, and re-layouts  17.4 us (16%)
  starting transfers between devices  12.7 us (12%)
  waiting for transfers between devices  12.4 us (12%)
  other arithmetic  6.19 us (6%)
    pallas_call x1, Pallas kernels, layers(): pl.pallas_call(functools.partial(layer_kernel, per_source, unique_count),...  36.7 us
    all_to_all x1, blocking collectives, shards(): lax.all_to_all(partial_sums, 'seq', split_axis=0, concat_axis=0, tiled=True)  8.41 us
    all_to_all x1, starting transfers between devices, shards(): lax.all_to_all(request, ('emb', 'seq'), split_axis=0, concat_axis=0, tile...  7.3 us
    all_to_all x1, waiting for transfers between devices, shards(): lax.all_to_all(outgoing_grads.astype(jnp.bfloat16), ('emb', 'seq'), split...  6.78 us
    all_gather x1, blocking collectives, shards(): shared = lax.all_gather(distinct_item_rows, 'seq', axis=0, tiled=True)  5.79 us
    all_gather x1, blocking collectives, shards(): group = lax.all_gather(packed, 'seq', axis=0, tiled=True)  5.23 us
    scatter x1, local copies, waits for them, and re-layouts, shards(): outgoing_grads = jnp.zeros((devices, slot_cap, feature), jnp.float32).at[...  3.72 us
    scatter x1, local copies, waits for them, and re-layouts, shards(): jnp.full((devices, slot_cap), rows_dev, jnp.int32).at[owners, slot_rank]  3.5 us
  transfers between devices with their start and end apart: 3, of which 3 were waited for; matrix products, arithmetic and copies ran while one was open for 6% of the time, Pallas kernels for 0%

profile of v2, /device:TPU:0, one launch (start us, length us, event | category | flops | bytes accessed | tf_op | source)
XLA Modules:
  0.0 105.6 jit_solution(14480325751239919788)
XLA Ops:
  0.6 0.8 and_select_fusion
  1.4 0.2 convert_reduce_fusion.1
  1.6 3.5 %scatter_fusion = s32[32,4]{0,1:T(4,128)S(1)} fusion(s32[32,4]{0,1:T(4,128)S(1)} %broadcast.85, s32[64]{0:T(128)S(1)} %get-tuple-element.11, s32[64]{0:T(128)S(1)} %get-tuple-element.12), kind=kCustom, calls=%fused_computation.2 | custom fusion | bytes 1280 | tf_op jit(solution)/shard_map/scatter | solution.py:242
  5.2 0.7 copy.34
  5.8 7.3 %all-to-all-start = ((s32[32,1,4]{2,1,0:T(1,128)}), s32[32,1,4]{2,1,0:T(1,128)S(1)}, u32[]{:S(2)}, u32[]{:S(2)}) async-start(s32[32,1,4]{2,1,0:T(1,128)} %copy.34), calls=%async_computation | async-start | bytes 32768 | tf_op jit(solution)/shard_map/all_to_all | solution.py:244
  13.2 0.7 slice.18
  13.8 0.8 slice.19
  14.6 0.7 copy.32
  15.3 0.7 copy.33
  16.1 0.2 reverse
  16.3 0.8 pad_add_fusion
  17.2 3.1 %all-to-all-done = s32[32,1,4]{2,1,0:T(1,128)S(1)} async-done(((s32[32,1,4]{2,1,0:T(1,128)}), s32[32,1,4]{2,1,0:T(1,128)S(1)}, u32[]{:S(2)}, u32[]{:S(2)}) %all-to-all-start) | async-done | bytes 544 | tf_op jit(solution)/shard_map/all_to_all | solution.py:244
  20.5 0.8 gather_fusion
  21.4 0.7 reshape.100
  22.1 2.8 %all-to-all-start.1 = ((bf16[32,4,512]{2,1,0:T(4,128)(2,1)}), bf16[32,4,512]{2,1,0:T(4,128)(2,1)S(1)}, u32[]{:S(2)}, u32[]{:S(2)}) async-start(bf16[32,4,512]{2,1,0:T(4,128)(2,1)} %reshape.100), calls=%async_computation.1 | async-start | bytes 262144 | tf_op jit(solution)/shard_map/all_to_all | solution.py:245
  24.9 5.2 %all_gather.6 = s32[32,258]{1,0:T(8,128)S(1)} all-gather(s32[8,258]{1,0:T(8,128)S(1)} %pad_add_fusion), channel_id=1, replica_groups=mesh['emb'=8,'seq'=4] {'seq'}, dimensions={0}, use_global_device_ids=true | all-gather | bytes 41280 | tf_op jit(solution)/shard_map/all_gather | solution.py:256
  30.1 0.2 slice_reduce_fusion
  30.3 0.2 fusion.4
  30.5 2.6 %all-to-all-done.1 = bf16[32,4,512]{2,1,0:T(4,128)(2,1)S(1)} async-done(((bf16[32,4,512]{2,1,0:T(4,128)(2,1)}), bf16[32,4,512]{2,1,0:T(4,128)(2,1)S(1)}, u32[]{:S(2)}, u32[]{:S(2)}) %all-to-all-start.1) | async-done | bytes 131104 | tf_op jit(solution)/shard_map/all_to_all | solution.py:245
  33.1 0.9 gather_fusion.1
  34.0 5.8 %all_gather.7.shared_ref = bf16[256,512]{1,0:T(8,128)(2,1)S(1)} all-gather(bf16[64,512]{1,0:T(8,128)(2,1)S(1)} %gather_fusion.1), channel_id=1, replica_groups=mesh['emb'=8,'seq'=4] {'seq'}, dimensions={0}, use_global_device_ids=true | all-gather | bytes 327680 | tf_op jit(solution)/shard_map/all_gather | solution.py:263
  39.8 1.6 %copy-done.2 = bf16[512,2048]{1,0:T(8,128)(2,1)S(1)} copy-done((bf16[512,2048]{1,0:T(8,128)(2,1)S(1)}, bf16[512,2048]{1,0:T(8,128)(2,1)}, u32[]{:S(2)}) %copy-start.2) | copy-done | bytes 2097176
  41.4 1.0 copy-done.3
  42.5 36.7 %shard_map.131 = (bf16[8,256,512]{2,1,0:T(8,128)(2,1)}, bf16[256,512]{1,0:T(8,128)(2,1)S(1)}) custom-call(s32[8]{0:T(128)S(1)} %get-tuple-element.9.sel_ref, s32[8]{0:T(128)S(1)} %get-tuple-element.8.len_ref, s32[32,1,256]{2,1,0:T(1,128)S(1)} %reshape.93.ids_ref, bf16[256,512]{1,0:T(8,128)(2,1)S(1)} %all_gather.7.shared_ref, ...), custom_call_target="tpu_custom_call" | custom-call | tf_op jit(solution)/shard_map/pallas_call | solution.py:174
  79.1 8.4 %all_to_all.28 = bf16[4,64,512]{2,1,0:T(8,128)(2,1)S(1)} all-to-all(bf16[4,64,512]{2,1,0:T(8,128)(2,1)S(1)} %bitcast.40), channel_id=1, replica_groups=mesh['emb'=8,'seq'=4] {'seq'}, dimensions={0} | all-to-all | bytes 524288 | tf_op jit(solution)/shard_map/all_to_all | solution.py:268
  87.6 3.7 %scatter_fusion.1 = f32[32,4,512]{2,1,0:T(4,128)S(1)} fusion(f32[32,4,512]{2,1,0:T(4,128)S(1)} %broadcast_in_dim.44, s32[64]{0:T(128)S(1)} %get-tuple-element.11, f32[64,512]{1,0:T(8,128)S(1)} %convert_reduce_fusion), kind=kCustom, calls=%fused_computation.3 | custom fusion | bytes 393728 | tf_op jit(solution)/shard_map/scatter | solution.py:275
  91.4 0.7 convert_element_type.13
  92.1 2.6 %all-to-all-start.3 = ((bf16[32,4,512]{2,1,0:T(4,128)(2,1)}), bf16[32,4,512]{2,1,0:T(4,128)(2,1)S(1)}, u32[]{:S(2)}, u32[]{:S(2)}) async-start(bf16[32,4,512]{2,1,0:T(4,128)(2,1)} %convert_element_type.13), calls=%async_computation.3 | async-start | bytes 262144 | tf_op jit(solution)/shard_map/all_to_all | solution.py:277
  94.6 0.6 broadcast.215
  95.2 0.7 reduce.7
  96.1 6.8 %all-to-all-done.3 = bf16[32,4,512]{2,1,0:T(4,128)(2,1)S(1)} async-done(((bf16[32,4,512]{2,1,0:T(4,128)(2,1)}), bf16[32,4,512]{2,1,0:T(4,128)(2,1)S(1)}, u32[]{:S(2)}, u32[]{:S(2)}) %all-to-all-start.3) | async-done | bytes 131104 | tf_op jit(solution)/shard_map/all_to_all | solution.py:277
  102.9 2.7 %scatter_custom_fusion.2 = f32[1024,512]{1,0:T(8,128)} fusion(s32[128]{0:T(128)S(1)} %fusion.7, f32[128,512]{1,0:T(8,128)S(1)} %reshape.129, f32[]{:T(128)} %constant.50.clone.1), kind=kCustom, calls=%fused_computation.5 | custom fusion | flops 65536 | bytes 2097156 | tf_op jit(solution)/shard_map/scatter-add | solution.py:283
  (29 shorter events, 0.7 us)
Async XLA Ops:
  0.6 19.9 %copy-start = (bf16[1024,512]{1,0:T(8,128)(2,1)S(1)}, bf16[1024,512]{1,0:T(8,128)(2,1)}, u32[]{:S(2)}) copy-start(bf16[1024,512]{1,0:T(8,128)(2,1)} %param.12) | copy-start | bytes 3145732
  1.6 38.2 %copy-start.1 = (bf16[8,256,512]{2,1,0:T(8,128)(2,1)S(1)}, bf16[8,256,512]{2,1,0:T(8,128)(2,1)}, u32[]{:S(2)}) copy-start(bf16[8,256,512]{2,1,0:T(8,128)(2,1)} %cot_ref.1) | copy-start | bytes 6291460
  1.6 38.2 %copy-start.4 = (f32[2048]{0:T(1024)S(1)}, f32[2048]{0:T(1024)}, u32[]{:S(2)}) copy-start(f32[2048]{0:T(1024)} %param.18) | copy-start | bytes 24580
  1.6 38.2 %copy-start.5 = (f32[512]{0:T(512)S(1)}, f32[512]{0:T(512)}, u32[]{:S(2)}) copy-start(f32[512]{0:T(512)} %param.19) | copy-start | bytes 6148
  1.6 38.2 %copy-start.6 = (f32[512]{0:T(512)S(1)}, f32[512]{0:T(512)}, u32[]{:S(2)}) copy-start(f32[512]{0:T(512)} %param.20) | copy-start | bytes 6148
  5.8 14.4 %all-to-all-start = ((s32[32,1,4]{2,1,0:T(1,128)}), s32[32,1,4]{2,1,0:T(1,128)S(1)}, u32[]{:S(2)}, u32[]{:S(2)}) async-start(s32[32,1,4]{2,1,0:T(1,128)} %copy.34), calls=%async_computation | async-start | bytes 32768 | tf_op jit(solution)/shard_map/all_to_all | solution.py:244
  22.1 11.0 %all-to-all-start.1 = ((bf16[32,4,512]{2,1,0:T(4,128)(2,1)}), bf16[32,4,512]{2,1,0:T(4,128)(2,1)S(1)}, u32[]{:S(2)}, u32[]{:S(2)}) async-start(bf16[32,4,512]{2,1,0:T(4,128)(2,1)} %reshape.100), calls=%async_computation.1 | async-start | bytes 262144 | tf_op jit(solution)/shard_map/all_to_all | solution.py:245
  39.8 1.6 %copy-start.2 = (bf16[512,2048]{1,0:T(8,128)(2,1)S(1)}, bf16[512,2048]{1,0:T(8,128)(2,1)}, u32[]{:S(2)}) copy-start(bf16[512,2048]{1,0:T(8,128)(2,1)} %proj_in_ref.1) | copy-start | bytes 6291460
  41.4 1.0 copy-start.3
  92.1 10.8 %all-to-all-start.3 = ((bf16[32,4,512]{2,1,0:T(4,128)(2,1)}), bf16[32,4,512]{2,1,0:T(4,128)(2,1)S(1)}, u32[]{:S(2)}, u32[]{:S(2)}) async-start(bf16[32,4,512]{2,1,0:T(4,128)(2,1)} %convert_element_type.13), calls=%async_computation.3 | async-start | bytes 262144 | tf_op jit(solution)/shard_map/all_to_all | solution.py:277

commit v3 on v2

v3 whole, which is shorter than its diff:
```python
import functools

import jax
import jax.numpy as jnp
from jax import lax
from jax.experimental import pallas as pl
from jax.experimental.pallas import tpu as pltpu
from jax.sharding import PartitionSpec as P


def nn(a, b):
    return lax.dot_general(a, b, (((1,), (0,)), ((), ())), preferred_element_type=jnp.float32)


def nt(a, b):
    return lax.dot_general(a, b, (((1,), (1,)), ((), ())), preferred_element_type=jnp.float32)


def tn(a, b):
    return lax.dot_general(a, b, (((0,), (0,)), ((), ())), preferred_element_type=jnp.float32)


def silu_parts(values):
    gate = 0.5 * jnp.tanh(0.5 * values) + 0.5
    out = values * gate
    return out, gate + out * (1.0 - gate)


def norm_parts(values):
    center = values - jnp.mean(values, axis=-1, keepdims=True)
    spread = jnp.mean(center * center, axis=-1, keepdims=True)
    scale = lax.rsqrt(spread + 1e-05)
    return center * scale, scale


def norm_pull(grad, unit, scale):
    first = jnp.mean(grad, axis=-1, keepdims=True)
    second = jnp.mean(grad * unit, axis=-1, keepdims=True)
    return scale * (grad - first - unit * second)


def layer_kernel(
    per_source,
    unique_count,
    bundle,
    sel_ref,
    len_ref,
    *refs,
):
    ids_refs = refs[:bundle]
    (
        shared_ref, cot_ref, proj_in_ref, bias_in_ref, gain_in_ref, gain_mid_ref, proj_out_ref,
        rev_ref, out_ref, part_ref, table, acc, hidden, slope, weights, wslope, mixed, dpre,
    ) = refs[bundle:]
    step = pl.program_id(0)
    head_count, max_len = rev_ref.shape
    feature = shared_ref.shape[1]
    head = feature // head_count
    width = shared_ref.shape[0]
    root = head ** (-0.5)
    slots = [step * bundle + b for b in range(bundle)]
    counts = [len_ref[t] for t in slots]
    longest = functools.reduce(jnp.maximum, counts)

    @pl.when(step == 0)
    def _():
        acc[...] = jnp.zeros_like(acc)
        for h in range(head_count):
            row = jnp.broadcast_to(rev_ref[h : h + 1, :], (max_len, max_len))
            table[h] = pltpu.roll(row, 0, 1, stride=1, stride_axis=0)

    def run(rows):
        total = bundle * rows
        spans = [slice(b * rows, (b + 1) * rows) for b in range(bundle)]
        place = lax.broadcasted_iota(jnp.int32, (1, rows), 1)
        ids = jnp.concatenate(
            [
                jnp.where(
                    place < n, ref[0, :, :rows] + sel_ref[t] // per_source * unique_count, -1
                )
                for ref, t, n in zip(ids_refs, slots, counts)
            ],
            axis=1,
        )
        chooser = jnp.where(
            lax.broadcasted_iota(jnp.int32, (width, total), 0) == ids, 1.0, 0.0
        ).astype(jnp.bfloat16)
        row = lax.broadcasted_iota(jnp.int32, (rows, 1), 0)
        valid = jnp.concatenate([(row < n).astype(jnp.float32) for n in counts], axis=0) > 0.5
        inputs = tn(chooser, shared_ref[...])
        unit_in, scale_in = norm_parts(inputs)
        normed = (unit_in * gain_in_ref[...]).astype(jnp.bfloat16)
        for c in (2, 3, 1, 0):
            cols = slice(c * feature, (c + 1) * feature)
            value, rate = silu_parts(nn(normed, proj_in_ref[:, cols]) + bias_in_ref[:, cols])
            hidden[:total, cols] = value.astype(jnp.bfloat16)
            slope[:total, cols] = rate.astype(jnp.bfloat16)
        causal = lax.broadcasted_iota(jnp.int32, (rows, rows), 1) <= lax.broadcasted_iota(
            jnp.int32, (rows, rows), 0
        )

        def part(c, h):
            return slice(c * feature + h * head, c * feature + (h + 1) * head)

        for b, span in enumerate(spans):
            share = 1.0 / jnp.full((1, 1), counts[b], jnp.int32).astype(jnp.float32)
            causal_share = jnp.where(causal, share, 0.0)
            for h in range(head_count):
                score = nt(hidden[span, part(2, h)], hidden[span, part(3, h)]) * root
                value, rate = silu_parts(score + table[h, :rows, :rows])
                weight = (value * causal_share).astype(jnp.bfloat16)
                weights[b, h, :rows, :rows] = weight
                wslope[b, h, :rows, :rows] = (rate * causal_share).astype(jnp.bfloat16)
                mixed[span, part(0, h)] = nn(weight, hidden[span, part(1, h)])
        unit_mid, scale_mid = norm_parts(mixed[:total, :])
        normed_mid = unit_mid * gain_mid_ref[...]
        gate = hidden[:total, :feature].astype(jnp.float32)
        gated = (normed_mid * gate).astype(jnp.bfloat16)
        result = inputs + nn(gated, proj_out_ref[...])
        result = jnp.where(valid, result, 0.0).astype(jnp.bfloat16)
        for b, span in enumerate(spans):
            out_ref[b, :rows, :] = result[span, :]
            if rows < max_len:
                out_ref[b, rows:, :] = jnp.zeros((max_len - rows, feature), jnp.bfloat16)

        grad = jnp.concatenate([cot_ref[b, :rows, :] for b in range(bundle)], axis=0)
        grad = jnp.where(valid, grad.astype(jnp.float32), 0.0)
        grad_gated = nt(grad.astype(jnp.bfloat16), proj_out_ref[...])
        grad_gated = grad_gated.astype(jnp.bfloat16).astype(jnp.float32)

        def put(span, cols, value):
            value = value.astype(jnp.bfloat16).astype(jnp.float32)
            dpre[span, cols] = (value * slope[span, cols].astype(jnp.float32)).astype(
                jnp.bfloat16
            )

        put(slice(0, total), slice(0, feature), grad_gated * normed_mid)
        grad_mixed = norm_pull(grad_gated * gate * gain_mid_ref[...], unit_mid, scale_mid)
        grad_mixed = grad_mixed.astype(jnp.bfloat16)
        for b, span in enumerate(spans):
            for h in range(head_count):
                grad_head = grad_mixed[span, h * head : (h + 1) * head]
                put(span, part(1, h), tn(weights[b, h, :rows, :rows], grad_head))
                grad_weight = nt(grad_head, hidden[span, part(1, h)])
                grad_score = (
                    grad_weight * wslope[b, h, :rows, :rows].astype(jnp.float32)
                ).astype(jnp.bfloat16)
                put(span, part(2, h), nn(grad_score, hidden[span, part(3, h)]) * root)
                put(span, part(3, h), tn(grad_score, hidden[span, part(2, h)]) * root)
        grad_normed = nt(dpre[:total, :], proj_in_ref[...])
        grad_normed = grad_normed.astype(jnp.bfloat16).astype(jnp.float32)
        grad_in = norm_pull(grad_normed * gain_in_ref[...], unit_in, scale_in)
        token_grad = (grad_in.astype(jnp.bfloat16).astype(jnp.float32) + grad).astype(jnp.bfloat16)
        acc[...] += nn(chooser, token_grad)

    half = max_len // 2

    @pl.when(longest <= half)
    def _():
        run(half)

    @pl.when(longest > half)
    def _():
        run(max_len)

    @pl.when(step == pl.num_programs(0) - 1)
    def _():
        part_ref[...] = acc[...].astype(part_ref.dtype)


def layers(
    selected, counts, ids, shared, cotangent, proj_in, bias_in, gain_in, gain_mid, proj_out, position_bias, per_source, unique_count, bundle
):
    slots, max_len, feature = cotangent.shape
    heads = position_bias.shape[0]
    width = shared.shape[0]
    rev = jnp.concatenate([position_bias[:, :1], position_bias[:, :0:-1]], axis=1)
    whole = lambda shape: pl.BlockSpec(shape, lambda t, sel, n: (0,) * len(shape))
    slot = pl.BlockSpec((bundle, max_len, feature), lambda t, sel, n: (t, 0, 0))
    ids = ids.reshape(ids.shape[0], 1, max_len)

    def chosen(b):
        return pl.BlockSpec((1, 1, max_len), lambda t, sel, n: (sel[t * bundle + b], 0, 0))
    return pl.pallas_call(
        functools.partial(layer_kernel, per_source, unique_count, bundle),
        grid_spec=pltpu.PrefetchScalarGridSpec(
            num_scalar_prefetch=2,
            grid=(slots // bundle,),
            in_specs=[
                *[chosen(b) for b in range(bundle)],
                whole((width, feature)),
                slot,
                whole(proj_in.shape),
                whole((1, bias_in.shape[0])),
                whole((1, feature)),
                whole((1, feature)),
                whole(proj_out.shape),
                whole((heads, max_len)),
            ],
            out_specs=[slot, whole((width, feature))],
            scratch_shapes=[
                pltpu.VMEM((heads, max_len, max_len), jnp.float32),
                pltpu.VMEM((width, feature), jnp.float32),
                pltpu.VMEM((bundle * max_len, 4 * feature), jnp.bfloat16),
                pltpu.VMEM((bundle * max_len, 4 * feature), jnp.bfloat16),
                pltpu.VMEM((bundle, heads, max_len, max_len), jnp.bfloat16),
                pltpu.VMEM((bundle, heads, max_len, max_len), jnp.bfloat16),
                pltpu.VMEM((bundle * max_len, feature), jnp.float32),
                pltpu.VMEM((bundle * max_len, 4 * feature), jnp.bfloat16),
            ],
        ),
        out_shape=[
            jax.ShapeDtypeStruct((slots, max_len, feature), jnp.bfloat16),
            jax.ShapeDtypeStruct((width, feature), jnp.bfloat16),
        ],
        compiler_params=pltpu.CompilerParams(
            dimension_semantics=("arbitrary",), vmem_limit_bytes=48 * 1024 * 1024
        ),
    )(
        selected, counts, *[ids] * bundle, shared, cotangent,
        proj_in, bias_in[None], gain_in[None], gain_mid[None], proj_out, rev,
    )


def shards(
    item_table,
    unique_ids,
    inverse,
    lengths,
    assignment,
    proj_in,
    bias_in,
    gain_in,
    gain_mid,
    proj_out,
    position_bias,
    cotangent,
):
    emb_count = lax.axis_size("emb")
    seq_count = lax.axis_size("seq")
    devices = emb_count * seq_count
    rows_dev = item_table.shape[0]
    feature = item_table.shape[1]
    unique_count = unique_ids.shape[0]
    slot_cap = 2 * unique_count // devices
    owners = unique_ids // rows_dev
    local_row = unique_ids % rows_dev
    order = jnp.arange(unique_count, dtype=jnp.int32)
    earlier = (owners[:, None] == owners[None, :]) & (order[None, :] < order[:, None])
    slot_rank = jnp.sum(earlier.astype(jnp.int32), axis=1)
    spot = owners * slot_cap + slot_rank
    spots = jnp.arange(devices * slot_cap, dtype=jnp.int32)
    placed = spots[:, None] == spot[None, :]
    request = rows_dev + jnp.sum(
        jnp.where(placed, local_row[None, :] - rows_dev, 0), axis=1
    ).reshape(devices, slot_cap)
    asked = lax.all_to_all(request, ("emb", "seq"), split_axis=0, concat_axis=0, tiled=True)
    answer = lax.all_to_all(
        item_table[jnp.minimum(asked, rows_dev - 1)],
        ("emb", "seq"),
        split_axis=0,
        concat_axis=0,
        tiled=True,
    )
    distinct_item_rows = answer[owners, slot_rank]
    slot_count = lengths.shape[0]
    max_len = inverse.shape[1]
    packed = jnp.concatenate([inverse, lengths[:, None], assignment[:, None]], axis=1)
    group = lax.all_gather(packed, "seq", axis=0, tiled=True)
    group_ids = group[:, :max_len]
    group_len = group[:, max_len]
    mine = lax.axis_index("seq") * slot_count + jnp.arange(slot_count, dtype=jnp.int32)
    hit = (group[:, max_len + 1][None, :] == mine[:, None]).astype(jnp.int32)
    selected = jnp.sum(hit * jnp.arange(hit.shape[1], dtype=jnp.int32)[None, :], axis=1)
    counts = jnp.sum(hit * group_len[None, :], axis=1)
    shared = lax.all_gather(distinct_item_rows, "seq", axis=0, tiled=True)
    outputs, partial_sums = layers(
        selected, counts, group_ids, shared, cotangent, proj_in, bias_in, gain_in, gain_mid,
        proj_out, position_bias, slot_count, unique_count, max(slot_count // seq_count, 1),
    )
    pieces = lax.all_to_all(partial_sums, "seq", split_axis=0, concat_axis=0, tiled=True)
    row_gradient_list = jnp.sum(
        pieces.reshape(seq_count, unique_count, feature).astype(jnp.float32), axis=0
    )
    outgoing_grads = jnp.dot(
        placed.astype(jnp.bfloat16),
        row_gradient_list.astype(jnp.bfloat16),
        preferred_element_type=jnp.float32,
    ).astype(jnp.bfloat16)
    landed = lax.all_to_all(
        outgoing_grads.reshape(devices, slot_cap, feature),
        ("emb", "seq"),
        split_axis=0,
        concat_axis=0,
        tiled=True,
    )
    holder = jnp.arange(rows_dev, dtype=jnp.int32)[:, None] == asked.reshape(1, -1)
    table_grad = jnp.dot(
        holder.astype(jnp.bfloat16),
        landed.reshape(-1, feature),
        preferred_element_type=jnp.float32,
    )
    return (outputs, table_grad)


def solution(mesh):
    in_specs = (
        P(("emb", "seq"), None),
        P(("emb", "seq")),
        P(("emb", "seq"), None),
        P(("emb", "seq")),
        P(("emb", "seq")),
        P(),
        P(),
        P(),
        P(),
        P(),
        P(),
        P(("emb", "seq"), None, None),
    )
    out_specs = (P(("emb", "seq"), None, None), P(("emb", "seq"), None))
    return jax.shard_map(shards, mesh=mesh, in_specs=in_specs, out_specs=out_specs, check_vma=False)
```

time: 106 us -> 96.5 us (0.910)
  Pallas kernels: 36.7 us -> 29.3 us
  local copies, waits for them, and re-layouts: 17.4 us -> 10.9 us
  other arithmetic: 6.19 us -> 2.93 us
  starting transfers between devices: 12.7 us -> 15.7 us
  waiting for transfers between devices: 12.4 us -> 14.9 us
  matrix products: 0 us -> 2.03 us
    pallas_call x1, Pallas kernels: 36.7 us -> 29.3 us  [layers(): pl.pallas_call(functools.partial(layer_kernel, per_source, unique_count,...]
    scatter x2 -> x0, local copies, waits for them, and re-layouts: 7.22 us -> none  [the longest x1 3.72 us: shards(): outgoing_grads = jnp.zeros((devices, slot_cap, feature), jnp.float32).at[...]
    all_to_all x1, waiting for transfers between devices: 2.59 us -> 8.1 us  [shards(): lax.all_to_all(item_table[jnp.minimum(asked, rows_dev - 1)], ('emb', 'seq...]
    all_to_all x1, waiting for transfers between devices: 3.07 us -> 0.01 us  [shards(): lax.all_to_all(request, ('emb', 'seq'), split_axis=0, concat_axis=0, tile...]
    all_to_all x1, starting transfers between devices: 2.77 us -> 5.83 us  [shards(): lax.all_to_all(item_table[jnp.minimum(asked, rows_dev - 1)], ('emb', 'seq...]
    scatter-add x1 -> x0, other arithmetic: 2.73 us -> none  [shards(): table_grad = jnp.zeros((rows_dev, feature), jnp.float32).at[asked.reshape...]
    dot_general x0 -> x2, matrix products: none -> 2.03 us  [the longest x1 1.74 us: shards(): jnp.dot(holder.astype(jnp.bfloat16), landed.reshape(-1, feature), preferr...]
  transfers between devices with their start and end apart: 3 -> 3, of which waited for: 3 -> 2; matrix products, arithmetic and copies ran while one was open for 6% -> 6% of each run, Pallas kernels for 0% -> 0%
where the time goes in v3:
time: 96.5 us; the launch traced here: 96 us
  Pallas kernels  29.3 us (30%)
  blocking collectives  19.4 us (20%)
  starting transfers between devices  15.7 us (16%)
  waiting for transfers between devices  14.9 us (15%)
  local copies, waits for them, and re-layouts  10.9 us (11%)
  other arithmetic  2.93 us (3%)
  matrix products  2.03 us (2%)
    pallas_call x1, Pallas kernels, layers(): pl.pallas_call(functools.partial(layer_kernel, per_source, unique_count,...  29.3 us
    all_to_all x1, blocking collectives, shards(): lax.all_to_all(partial_sums, 'seq', split_axis=0, concat_axis=0, tiled=True)  8.41 us
    all_to_all x1, waiting for transfers between devices, shards(): lax.all_to_all(item_table[jnp.minimum(asked, rows_dev - 1)], ('emb', 'seq...  8.1 us
    all_to_all x1, starting transfers between devices, shards(): lax.all_to_all(request, ('emb', 'seq'), split_axis=0, concat_axis=0, tile...  7.3 us
    all_to_all x1, waiting for transfers between devices, shards(): lax.all_to_all(outgoing_grads.reshape(devices, slot_cap, feature), ('emb'...  6.79 us
    all_to_all x1, starting transfers between devices, shards(): lax.all_to_all(item_table[jnp.minimum(asked, rows_dev - 1)], ('emb', 'seq...  5.83 us
    all_gather x1, blocking collectives, shards(): shared = lax.all_gather(distinct_item_rows, 'seq', axis=0, tiled=True)  5.79 us
    all_gather x1, blocking collectives, shards(): group = lax.all_gather(packed, 'seq', axis=0, tiled=True)  5.21 us
  transfers between devices with their start and end apart: 3, of which 2 were waited for; matrix products, arithmetic and copies ran while one was open for 6% of the time, Pallas kernels for 0%

profile of v3, /device:TPU:0, one launch (start us, length us, event | category | flops | bytes accessed | tf_op | source)
XLA Modules:
  0.0 96.0 jit_solution(2621297915268092998)
XLA Ops:
  0.7 0.8 and_select_fusion.1
  1.5 0.2 convert_reduce_fusion
  1.7 0.1 select_reduce_fusion
  1.8 0.7 add.66
  2.5 7.3 %all-to-all-start = ((s32[32,1,4]{2,1,0:T(1,128)}), s32[32,1,4]{2,1,0:T(1,128)S(1)}, u32[]{:S(2)}, u32[]{:S(2)}) async-start(s32[32,1,4]{2,1,0:T(1,128)} %bitcast.2), calls=%async_computation | async-start | bytes 32768 | tf_op jit(solution)/shard_map/all_to_all | solution.py:257
  9.8 0.7 copy.32
  10.6 0.7 copy.33
  11.3 0.8 pad_add_fusion
  12.1 5.2 %all_gather.6 = s32[32,258]{1,0:T(8,128)S(1)} all-gather(s32[8,258]{1,0:T(8,128)S(1)} %pad_add_fusion), channel_id=1, replica_groups=mesh['emb'=8,'seq'=4] {'seq'}, dimensions={0}, use_global_device_ids=true | all-gather | bytes 41280 | tf_op jit(solution)/shard_map/all_gather | solution.py:269
  17.3 0.2 slice_reduce_fusion
  17.5 0.2 fusion.5
  17.6 0.7 slice.18
  18.3 0.8 slice.19
  19.1 0.2 reverse
  19.5 0.1 reshape.85
  19.7 0.8 gather_fusion
  20.5 0.7 reshape.84
  21.2 5.8 %all-to-all-start.1 = ((bf16[32,4,512]{2,1,0:T(4,128)(2,1)}), bf16[32,4,512]{2,1,0:T(4,128)(2,1)S(1)}, u32[]{:S(2)}, u32[]{:S(2)}) async-start(bf16[32,4,512]{2,1,0:T(4,128)(2,1)} %reshape.84), calls=%async_computation.1 | async-start | bytes 262144 | tf_op jit(solution)/shard_map/all_to_all | solution.py:258
  27.2 8.1 %all-to-all-done.1 = bf16[32,4,512]{2,1,0:T(4,128)(2,1)S(1)} async-done(((bf16[32,4,512]{2,1,0:T(4,128)(2,1)}), bf16[32,4,512]{2,1,0:T(4,128)(2,1)S(1)}, u32[]{:S(2)}, u32[]{:S(2)}) %all-to-all-start.1) | async-done | bytes 131104 | tf_op jit(solution)/shard_map/all_to_all | solution.py:258
  35.3 0.9 gather_fusion.1
  36.2 5.8 %all_gather.7.refs_2_ = bf16[256,512]{1,0:T(8,128)(2,1)S(1)} all-gather(bf16[64,512]{1,0:T(8,128)(2,1)S(1)} %gather_fusion.1), channel_id=1, replica_groups=mesh['emb'=8,'seq'=4] {'seq'}, dimensions={0}, use_global_device_ids=true | all-gather | bytes 327680 | tf_op jit(solution)/shard_map/all_gather | solution.py:276
  42.0 1.6 %copy-done.2 = bf16[512,2048]{1,0:T(8,128)(2,1)S(1)} copy-done((bf16[512,2048]{1,0:T(8,128)(2,1)S(1)}, bf16[512,2048]{1,0:T(8,128)(2,1)}, u32[]{:S(2)}) %copy-start.2) | copy-done | bytes 2097176
  43.6 1.0 %copy-done.3 = bf16[512,512]{1,0:T(8,128)(2,1)S(1)} copy-done((bf16[512,512]{1,0:T(8,128)(2,1)S(1)}, bf16[512,512]{1,0:T(8,128)(2,1)}, u32[]{:S(2)}) %copy-start.3) | copy-done | bytes 524312
  44.7 29.3 %shard_map.131 = (bf16[8,256,512]{2,1,0:T(8,128)(2,1)}, bf16[256,512]{1,0:T(8,128)(2,1)S(1)}) custom-call(s32[8]{0:T(128)S(1)} %get-tuple-element.9.sel_ref, s32[8]{0:T(128)S(1)} %get-tuple-element.8.len_ref, s32[32,1,256]{2,1,0:T(1,128)S(1)} %reshape.80.refs_0_.refs_1_, s32[32,1,256]{2,1,0:T(1,128)S(1)} %reshape.80.refs_0_.refs_1_, ...), custom_call_target="tpu_custom_call" | custom-call | tf_op jit(solution)/shard_map/pallas_call | solution.py:184
  74.0 8.4 %all_to_all.25 = bf16[4,64,512]{2,1,0:T(8,128)(2,1)S(1)} all-to-all(bf16[4,64,512]{2,1,0:T(8,128)(2,1)S(1)} %bitcast.26), channel_id=1, replica_groups=mesh['emb'=8,'seq'=4] {'seq'}, dimensions={0} | all-to-all | bytes 524288 | tf_op jit(solution)/shard_map/all_to_all | solution.py:281
  82.4 0.3 convolution_convert_fusion
  82.7 0.7 reshape.81
  83.4 2.6 %all-to-all-start.3 = ((bf16[32,4,512]{2,1,0:T(4,128)(2,1)}), bf16[32,4,512]{2,1,0:T(4,128)(2,1)S(1)}, u32[]{:S(2)}, u32[]{:S(2)}) async-start(bf16[32,4,512]{2,1,0:T(4,128)(2,1)} %reshape.81), calls=%async_computation.3 | async-start | bytes 262144 | tf_op jit(solution)/shard_map/all_to_all | solution.py:290
  86.0 0.6 broadcast.143
  86.6 0.7 reduce.9
  87.4 6.8 %all-to-all-done.3 = bf16[32,4,512]{2,1,0:T(4,128)(2,1)S(1)} async-done(((bf16[32,4,512]{2,1,0:T(4,128)(2,1)}), bf16[32,4,512]{2,1,0:T(4,128)(2,1)S(1)}, u32[]{:S(2)}, u32[]{:S(2)}) %all-to-all-start.3) | async-done | bytes 131104 | tf_op jit(solution)/shard_map/all_to_all | solution.py:290
  94.3 1.7 %fusion = f32[1024,512]{1,0:T(8,128)} fusion(bf16[128,512]{1,0:T(8,128)(2,1)S(1)} %reshape.82, s32[128]{0:T(128)S(1)} %eq.69), kind=kOutput, calls=%fused_computation.4 | convolution fusion | flops 134348800 | bytes 2228736 | tf_op jit(solution)/shard_map/dot_general | solution.py:298
  (28 shorter events, 0.6 us)
Async XLA Ops:
  0.6 19.0 %copy-start = (bf16[1024,512]{1,0:T(8,128)(2,1)S(1)}, bf16[1024,512]{1,0:T(8,128)(2,1)}, u32[]{:S(2)}) copy-start(bf16[1024,512]{1,0:T(8,128)(2,1)} %param.12) | copy-start | bytes 3145732
  0.6 41.4 %copy-start.1 = (bf16[8,256,512]{2,1,0:T(8,128)(2,1)S(1)}, bf16[8,256,512]{2,1,0:T(8,128)(2,1)}, u32[]{:S(2)}) copy-start(bf16[8,256,512]{2,1,0:T(8,128)(2,1)} %refs_3_.1) | copy-start | bytes 6291460
  0.7 41.4 %copy-start.6 = (f32[512]{0:T(512)S(1)}, f32[512]{0:T(512)}, u32[]{:S(2)}) copy-start(f32[512]{0:T(512)} %param.20) | copy-start | bytes 6148
  0.7 41.3 %copy-start.5 = (f32[512]{0:T(512)S(1)}, f32[512]{0:T(512)}, u32[]{:S(2)}) copy-start(f32[512]{0:T(512)} %param.19) | copy-start | bytes 6148
  0.7 41.3 %copy-start.4 = (f32[2048]{0:T(1024)S(1)}, f32[2048]{0:T(1024)}, u32[]{:S(2)}) copy-start(f32[2048]{0:T(1024)} %param.18) | copy-start | bytes 24580
  2.5 16.8 %all-to-all-start = ((s32[32,1,4]{2,1,0:T(1,128)}), s32[32,1,4]{2,1,0:T(1,128)S(1)}, u32[]{:S(2)}, u32[]{:S(2)}) async-start(s32[32,1,4]{2,1,0:T(1,128)} %bitcast.2), calls=%async_computation | async-start | bytes 32768 | tf_op jit(solution)/shard_map/all_to_all | solution.py:257
  21.2 14.1 %all-to-all-start.1 = ((bf16[32,4,512]{2,1,0:T(4,128)(2,1)}), bf16[32,4,512]{2,1,0:T(4,128)(2,1)S(1)}, u32[]{:S(2)}, u32[]{:S(2)}) async-start(bf16[32,4,512]{2,1,0:T(4,128)(2,1)} %reshape.84), calls=%async_computation.1 | async-start | bytes 262144 | tf_op jit(solution)/shard_map/all_to_all | solution.py:258
  42.0 1.6 %copy-start.2 = (bf16[512,2048]{1,0:T(8,128)(2,1)S(1)}, bf16[512,2048]{1,0:T(8,128)(2,1)}, u32[]{:S(2)}) copy-start(bf16[512,2048]{1,0:T(8,128)(2,1)} %refs_4_.1) | copy-start | bytes 6291460
  43.6 1.0 %copy-start.3 = (bf16[512,512]{1,0:T(8,128)(2,1)S(1)}, bf16[512,512]{1,0:T(8,128)(2,1)}, u32[]{:S(2)}) copy-start(bf16[512,512]{1,0:T(8,128)(2,1)} %refs_8_.1) | copy-start | bytes 1572868
  83.4 10.8 %all-to-all-start.3 = ((bf16[32,4,512]{2,1,0:T(4,128)(2,1)}), bf16[32,4,512]{2,1,0:T(4,128)(2,1)S(1)}, u32[]{:S(2)}, u32[]{:S(2)}) async-start(bf16[32,4,512]{2,1,0:T(4,128)(2,1)} %reshape.81), calls=%async_computation.3 | async-start | bytes 262144 | tf_op jit(solution)/shard_map/all_to_all | solution.py:290

commit v4 on v3

--- a/solution.py
+++ b/solution.py
@@ -265,15 +265,21 @@
     distinct_item_rows = answer[owners, slot_rank]
     slot_count = lengths.shape[0]
     max_len = inverse.shape[1]
-    packed = jnp.concatenate([inverse, lengths[:, None], assignment[:, None]], axis=1)
-    group = lax.all_gather(packed, "seq", axis=0, tiled=True)
-    group_ids = group[:, :max_len]
-    group_len = group[:, max_len]
+    numbers = jnp.concatenate([inverse.reshape(-1), lengths, assignment]).astype(jnp.bfloat16)
+    extra = -(-numbers.shape[0] // (16 * feature)) * 16
+    numbers = jnp.pad(numbers, (0, extra * feature - numbers.shape[0]))
+    packed = jnp.concatenate([distinct_item_rows, numbers.reshape(extra, feature)], axis=0)
+    group = lax.all_gather(packed, "seq", axis=0, tiled=False)
+    shared = group[:, :unique_count].reshape(seq_count * unique_count, feature)
+    numbers = group[:, unique_count:].reshape(seq_count, extra * feature).astype(jnp.int32)
+    tokens = slot_count * max_len
+    group_ids = numbers[:, :tokens].reshape(seq_count * slot_count, max_len)
+    group_len = numbers[:, tokens : tokens + slot_count].reshape(-1)
+    group_place = numbers[:, tokens + slot_count : tokens + 2 * slot_count].reshape(-1)
     mine = lax.axis_index("seq") * slot_count + jnp.arange(slot_count, dtype=jnp.int32)
-    hit = (group[:, max_len + 1][None, :] == mine[:, None]).astype(jnp.int32)
+    hit = (group_place[None, :] == mine[:, None]).astype(jnp.int32)
     selected = jnp.sum(hit * jnp.arange(hit.shape[1], dtype=jnp.int32)[None, :], axis=1)
     counts = jnp.sum(hit * group_len[None, :], axis=1)
-    shared = lax.all_gather(distinct_item_rows, "seq", axis=0, tiled=True)
     outputs, partial_sums = layers(
         selected, counts, group_ids, shared, cotangent, proj_in, bias_in, gain_in, gain_mid,
         proj_out, position_bias, slot_count, unique_count, max(slot_count // seq_count, 1),

time: 96.5 us -> 91.5 us (0.948)
  blocking collectives: 19.4 us -> 14.5 us
  starting transfers between devices: 15.7 us -> 12.4 us
  waiting for transfers between devices: 14.9 us -> 18.1 us
  other arithmetic: 2.93 us -> 4.15 us
  local copies, waits for them, and re-layouts: 10.9 us -> 9.75 us
    all_gather x2 -> x1, blocking collectives: 11 us -> 6.09 us  [shards(): group = lax.all_gather(packed, 'seq', axis=0, tiled=False)]
    all_to_all x1, waiting for transfers between devices: 0.01 us -> 4.59 us  [shards(): lax.all_to_all(request, ('emb', 'seq'), split_axis=0, concat_axis=0, tile...]
    all_to_all x1, starting transfers between devices: 5.83 us -> 2.58 us  [shards(): lax.all_to_all(item_table[jnp.minimum(asked, rows_dev - 1)], ('emb', 'seq...]
    broadcast_in_dim x2 -> x0, local copies, waits for them, and re-layouts: 1.46 us -> none  [the longest x1 0.73 us: shards(): lengths[:, None]]
    all_to_all x1, waiting for transfers between devices: 8.1 us -> 6.75 us  [shards(): lax.all_to_all(item_table[jnp.minimum(asked, rows_dev - 1)], ('emb', 'seq...]
    another operation x0 -> x2, other arithmetic: none -> 1.32 us
    unnamed x16 -> x18, local copies, waits for them, and re-layouts: 2.91 us -> 3 us
  transfers between devices with their start and end apart: 3 -> 3, of which waited for: 2 -> 3; matrix products, arithmetic and copies ran while one was open for 6% -> 6% of each run, Pallas kernels for 0% -> 0%
where the time goes in v4:
time: 91.5 us; the launch traced here: 91 us
  Pallas kernels  29.1 us (32%)
  waiting for transfers between devices  18.1 us (20%)
  blocking collectives  14.5 us (16%)
  starting transfers between devices  12.4 us (14%)
  local copies, waits for them, and re-layouts  9.75 us (11%)
  other arithmetic  4.15 us (5%)
  matrix products  2.03 us (2%)
    pallas_call x1, Pallas kernels, layers(): pl.pallas_call(functools.partial(layer_kernel, per_source, unique_count,...  29.1 us
    all_to_all x1, blocking collectives, shards(): lax.all_to_all(partial_sums, 'seq', split_axis=0, concat_axis=0, tiled=True)  8.41 us
    all_to_all x1, starting transfers between devices, shards(): lax.all_to_all(request, ('emb', 'seq'), split_axis=0, concat_axis=0, tile...  7.3 us
    all_to_all x1, waiting for transfers between devices, shards(): lax.all_to_all(outgoing_grads.reshape(devices, slot_cap, feature), ('emb'...  6.79 us
    all_to_all x1, waiting for transfers between devices, shards(): lax.all_to_all(item_table[jnp.minimum(asked, rows_dev - 1)], ('emb', 'seq...  6.75 us
    all_gather x1, blocking collectives, shards(): group = lax.all_gather(packed, 'seq', axis=0, tiled=False)  6.09 us
    all_to_all x1, waiting for transfers between devices, shards(): lax.all_to_all(request, ('emb', 'seq'), split_axis=0, concat_axis=0, tile...  4.59 us
    unnamed x18, local copies, waits for them, and re-layouts  3 us
  transfers between devices with their start and end apart: 3, of which 3 were waited for; matrix products, arithmetic and copies ran while one was open for 6% of the time, Pallas kernels for 0%

profile of v4, /device:TPU:0, one launch (start us, length us, event | category | flops | bytes accessed | tf_op | source)
XLA Modules:
  0.0 91.0 jit_solution(16115413253624752330)
XLA Ops:
  0.6 0.8 and_select_fusion.1
  1.4 0.2 convert_reduce_fusion
  1.6 0.1 select_reduce_fusion
  1.7 0.7 add.66
  2.4 7.3 %all-to-all-start = ((s32[32,1,4]{2,1,0:T(1,128)}), s32[32,1,4]{2,1,0:T(1,128)S(1)}, u32[]{:S(2)}, u32[]{:S(2)}) async-start(s32[32,1,4]{2,1,0:T(1,128)} %bitcast), calls=%async_computation | async-start | bytes 32768 | tf_op jit(solution)/shard_map/all_to_all | solution.py:257
  9.7 0.7 slice.26
  10.4 0.8 slice.27
  11.2 0.7 convert_bitcast_fusion.1
  11.9 0.2 reverse
  12.2 4.6 %all-to-all-done = s32[32,1,4]{2,1,0:T(1,128)S(1)} async-done(((s32[32,1,4]{2,1,0:T(1,128)}), s32[32,1,4]{2,1,0:T(1,128)S(1)}, u32[]{:S(2)}, u32[]{:S(2)}) %all-to-all-start) | async-done | bytes 544 | tf_op jit(solution)/shard_map/all_to_all | solution.py:257
  17.0 0.1 reshape.98
  17.1 0.8 gather_fusion
  18.0 0.7 reshape.97
  18.7 2.6 %all-to-all-start.1 = ((bf16[32,4,512]{2,1,0:T(4,128)(2,1)}), bf16[32,4,512]{2,1,0:T(4,128)(2,1)S(1)}, u32[]{:S(2)}, u32[]{:S(2)}) async-start(bf16[32,4,512]{2,1,0:T(4,128)(2,1)} %reshape.97), calls=%async_computation.1 | async-start | bytes 262144 | tf_op jit(solution)/shard_map/all_to_all | solution.py:258
  21.3 0.7 convert.13
  21.9 0.7 convert.14
  22.7 6.7 %all-to-all-done.1 = bf16[32,4,512]{2,1,0:T(4,128)(2,1)S(1)} async-done(((bf16[32,4,512]{2,1,0:T(4,128)(2,1)}), bf16[32,4,512]{2,1,0:T(4,128)(2,1)S(1)}, u32[]{:S(2)}, u32[]{:S(2)}) %all-to-all-start.1) | async-done | bytes 131104 | tf_op jit(solution)/shard_map/all_to_all | solution.py:258
  29.5 0.9 %gather_fusion.1 = bf16[64,512]{1,0:T(8,128)(2,1)S(1)} fusion(bf16[32,4,512]{2,1,0:T(4,128)(2,1)S(1)} %all-to-all-done.1, s32[64]{0:T(128)S(1)} %fusion.13), kind=kCustom, calls=%fused_computation.1 | custom fusion | bytes 131584 | tf_op jit(solution)/shard_map/gather | solution.py:265
  30.4 6.1 %all-gather = bf16[320,512]{1,0:T(8,128)(2,1)S(1)} all-gather(bf16[80,512]{1,0:T(8,128)(2,1)S(1)} %pad_maximum_fusion), channel_id=2, replica_groups=mesh['emb'=8,'seq'=4] {'seq'}, dimensions={0}, use_global_device_ids=true | all-gather | bytes 409600 | tf_op jit(solution)/shard_map/all_gather | solution.py:272
  37.0 0.2 fusion.5
  37.2 1.6 %copy-done.2 = bf16[512,2048]{1,0:T(8,128)(2,1)S(1)} copy-done((bf16[512,2048]{1,0:T(8,128)(2,1)S(1)}, bf16[512,2048]{1,0:T(8,128)(2,1)}, u32[]{:S(2)}) %copy-start.2) | copy-done | bytes 2097176
  38.8 1.0 %copy-done.3 = bf16[512,512]{1,0:T(8,128)(2,1)S(1)} copy-done((bf16[512,512]{1,0:T(8,128)(2,1)S(1)}, bf16[512,512]{1,0:T(8,128)(2,1)}, u32[]{:S(2)}) %copy-start.3) | copy-done | bytes 524312
  39.8 29.1 %shard_map.131 = (bf16[8,256,512]{2,1,0:T(8,128)(2,1)}, bf16[256,512]{1,0:T(8,128)(2,1)S(1)}) custom-call(s32[8]{0:T(128)S(1)} %get-tuple-element.7.sel_ref, s32[8]{0:T(128)S(1)} %get-tuple-element.6.len_ref, s32[32,1,256]{2,1,0:T(1,128)S(1)} %reshape_reshape.3.refs_0_.refs_1_, s32[32,1,256]{2,1,0:T(1,128)S(1)} %reshape_reshape.3.refs_0_.refs_1_, ...), custom_call_target="tpu_custom_call" | custom-call | tf_op jit(solution)/shard_map/pallas_call | solution.py:184
  68.9 8.4 %all_to_all.25 = bf16[4,64,512]{2,1,0:T(8,128)(2,1)S(1)} all-to-all(bf16[4,64,512]{2,1,0:T(8,128)(2,1)S(1)} %bitcast.33), channel_id=1, replica_groups=mesh['emb'=8,'seq'=4] {'seq'}, dimensions={0} | all-to-all | bytes 524288 | tf_op jit(solution)/shard_map/all_to_all | solution.py:287
  77.4 0.3 convolution_convert_fusion
  77.7 0.7 reshape.93
  78.4 2.6 %all-to-all-start.3 = ((bf16[32,4,512]{2,1,0:T(4,128)(2,1)}), bf16[32,4,512]{2,1,0:T(4,128)(2,1)S(1)}, u32[]{:S(2)}, u32[]{:S(2)}) async-start(bf16[32,4,512]{2,1,0:T(4,128)(2,1)} %reshape.93), calls=%async_computation.3 | async-start | bytes 262144 | tf_op jit(solution)/shard_map/all_to_all | solution.py:296
  81.0 0.6 broadcast.143
  81.6 0.7 reduce.5
  82.3 0.1 eq.69
  82.4 6.8 %all-to-all-done.3 = bf16[32,4,512]{2,1,0:T(4,128)(2,1)S(1)} async-done(((bf16[32,4,512]{2,1,0:T(4,128)(2,1)}), bf16[32,4,512]{2,1,0:T(4,128)(2,1)S(1)}, u32[]{:S(2)}, u32[]{:S(2)}) %all-to-all-start.3) | async-done | bytes 131104 | tf_op jit(solution)/shard_map/all_to_all | solution.py:296
  89.2 1.7 %fusion = f32[1024,512]{1,0:T(8,128)} fusion(bf16[128,512]{1,0:T(8,128)(2,1)S(1)} %reshape.94, s32[128]{0:T(128)S(1)} %eq.69), kind=kOutput, calls=%fused_computation.4 | convolution fusion | flops 134348800 | bytes 2228736 | tf_op jit(solution)/shard_map/dot_general | solution.py:304
  (37 shorter events, 1.0 us)
Async XLA Ops:
  0.6 16.5 %copy-start = (bf16[1024,512]{1,0:T(8,128)(2,1)S(1)}, bf16[1024,512]{1,0:T(8,128)(2,1)}, u32[]{:S(2)}) copy-start(bf16[1024,512]{1,0:T(8,128)(2,1)} %param.12) | copy-start | bytes 3145732
  2.4 14.4 %all-to-all-start = ((s32[32,1,4]{2,1,0:T(1,128)}), s32[32,1,4]{2,1,0:T(1,128)S(1)}, u32[]{:S(2)}, u32[]{:S(2)}) async-start(s32[32,1,4]{2,1,0:T(1,128)} %bitcast), calls=%async_computation | async-start | bytes 32768 | tf_op jit(solution)/shard_map/all_to_all | solution.py:257
  16.9 20.3 %copy-start.1 = (bf16[8,256,512]{2,1,0:T(8,128)(2,1)S(1)}, bf16[8,256,512]{2,1,0:T(8,128)(2,1)}, u32[]{:S(2)}) copy-start(bf16[8,256,512]{2,1,0:T(8,128)(2,1)} %refs_3_.1) | copy-start | bytes 6291460
  16.9 20.3 %copy-start.4 = (f32[2048]{0:T(1024)S(1)}, f32[2048]{0:T(1024)}, u32[]{:S(2)}) copy-start(f32[2048]{0:T(1024)} %param.18) | copy-start | bytes 24580
  16.9 20.3 %copy-start.5 = (f32[512]{0:T(512)S(1)}, f32[512]{0:T(512)}, u32[]{:S(2)}) copy-start(f32[512]{0:T(512)} %param.19) | copy-start | bytes 6148
  16.9 20.3 %copy-start.6 = (f32[512]{0:T(512)S(1)}, f32[512]{0:T(512)}, u32[]{:S(2)}) copy-start(f32[512]{0:T(512)} %param.20) | copy-start | bytes 6148
  18.7 10.8 %all-to-all-start.1 = ((bf16[32,4,512]{2,1,0:T(4,128)(2,1)}), bf16[32,4,512]{2,1,0:T(4,128)(2,1)S(1)}, u32[]{:S(2)}, u32[]{:S(2)}) async-start(bf16[32,4,512]{2,1,0:T(4,128)(2,1)} %reshape.97), calls=%async_computation.1 | async-start | bytes 262144 | tf_op jit(solution)/shard_map/all_to_all | solution.py:258
  37.2 1.6 %copy-start.2 = (bf16[512,2048]{1,0:T(8,128)(2,1)S(1)}, bf16[512,2048]{1,0:T(8,128)(2,1)}, u32[]{:S(2)}) copy-start(bf16[512,2048]{1,0:T(8,128)(2,1)} %refs_4_.1) | copy-start | bytes 6291460
  38.8 1.0 %copy-start.3 = (bf16[512,512]{1,0:T(8,128)(2,1)S(1)}, bf16[512,512]{1,0:T(8,128)(2,1)}, u32[]{:S(2)}) copy-start(bf16[512,512]{1,0:T(8,128)(2,1)} %refs_8_.1) | copy-start | bytes 1572868
  78.4 10.8 %all-to-all-start.3 = ((bf16[32,4,512]{2,1,0:T(4,128)(2,1)}), bf16[32,4,512]{2,1,0:T(4,128)(2,1)S(1)}, u32[]{:S(2)}, u32[]{:S(2)}) async-start(bf16[32,4,512]{2,1,0:T(4,128)(2,1)} %reshape.93), calls=%async_computation.3 | async-start | bytes 262144 | tf_op jit(solution)/shard_map/all_to_all | solution.py:296
